TPU v7x, 128 devices: a whole 4x4x4 slice. The times are simulated.
128 devices in a mesh: src: 8 (over z_lo, y), tgt: 16 (over x, z_hi, core).
Axes of the slice: x: 4, y: 4, z: 4 (z_hi: 2, z_lo: 2; z = z_hi * 2 + z_lo), core: 2. Of those that a mesh axis runs over, the one named last changes fastest.
Arguments:
- charges: bfloat16 [2, 512, 1024, 512], P(None, ('src', 'tgt')), may hold values from -6 to 6
- source_xy: float32 [2, 512, 1024], P(None, ('src', 'tgt')), may hold values from 0 to 8
- target_xy: float32 [2, 128, 1024], P(None, ('src', 'tgt')), may hold values from 0 to 8
- anterp: bfloat16 [2, 512, 128, 1024], P(None, ('src', 'tgt')), may hold values from -0.1875 to 0.1875
- levels: bfloat16 [2, 2, 2, 512, 128, 128], P(None, None, None, ('src', 'tgt')), may hold values from -0.375 to 0.375
- transfer: bfloat16 [2, 128, 128, 8192], P(None, ('src', 'tgt')), may hold values from -0.0625 to 0.0625
- evaluate: bfloat16 [2, 128, 1024, 128], P(None, ('src', 'tgt')), may hold values from -0.5 to 0.5
- near_list: int32 [128, 3], P(('src', 'tgt')), may hold values from 0 to 3
Outputs:
- field: float32 [2, 128, 1024, 512], P(None, ('src', 'tgt'))
Inputs may be any that keep to these rules, and one draw needn't show every extreme that they name: near_list[g, k] names one of the 4 source blocks of the device k - 1 columns further along tgt in g's quadtree row; entries naming a column outside the grid are ignored.
All inputs are finite; a program needn't handle non-finite values.
Results may differ from a plain program's by a relative error of at most 0.0065.
Values may be sent and summed in bfloat16 or wider, within the bound.
A program may use at most 256 MiB of HBM per device.

v0:
```python
import jax
import jax.numpy as jnp
from jax import lax
from jax.sharding import PartitionSpec as P

KAPPA = 73.27
CORE = 0.5
BOX = 8.0


def from_partner(array, axis, apart):
    return lax.ppermute(array, axis, [(i, i ^ 1 << apart) for i in range(lax.axis_size(axis))])


def extended(array, sides, width):
    for axis, dim in sides:
        peers, length = (lax.axis_size(axis), array.shape[dim])
        up = [(i, (i + 1) % peers) for i in range(peers - 1)]
        down = [(j, i) for i, j in up]
        last = lax.slice_in_dim(array, length - width, length, axis=dim)
        first = lax.slice_in_dim(array, 0, width, axis=dim)
        before = lax.ppermute(last, axis, up)
        after = lax.ppermute(first, axis, down)
        array = jnp.concatenate([before, array, after], axis=dim)
    return array


def complex_apply(matrix, vector, form):
    real_part = jnp.einsum(
        form, matrix[0], vector[0], preferred_element_type=jnp.float32
    ) - jnp.einsum(form, matrix[1], vector[1], preferred_element_type=jnp.float32)
    imag_part = jnp.einsum(
        form, matrix[0], vector[1], preferred_element_type=jnp.float32
    ) + jnp.einsum(form, matrix[1], vector[0], preferred_element_type=jnp.float32)
    return jnp.stack([real_part, imag_part])


def kernel_term(target_pos, source_pos, strengths):
    delta_x = target_pos[0][:, None] - source_pos[0][None, :]
    delta_y = target_pos[1][:, None] - source_pos[1][None, :]
    distance = jnp.sqrt(delta_x * delta_x + delta_y * delta_y + CORE * CORE)
    amplitude = 1.0 / (4.0 * jnp.pi * distance)
    phase = KAPPA * distance
    cosine = (amplitude * jnp.cos(phase)).astype(jnp.bfloat16)
    sine = (amplitude * jnp.sin(phase)).astype(jnp.bfloat16)
    real_part = jnp.dot(cosine, strengths[0], preferred_element_type=jnp.float32) - jnp.dot(
        sine, strengths[1], preferred_element_type=jnp.float32
    )
    imag_part = jnp.dot(cosine, strengths[1], preferred_element_type=jnp.float32) + jnp.dot(
        sine, strengths[0], preferred_element_type=jnp.float32
    )
    return jnp.stack([real_part, imag_part])


def shards(charges, source_xy, target_xy, anterp, levels, transfer, evaluate, near_list):
    source_blocks = charges.shape[1]
    rank = anterp.shape[2]
    columns = charges.shape[3]
    coeff = complex_apply(anterp, charges, "bij,bjn->bin").astype(jnp.bfloat16)
    top_bit = lax.axis_size("src").bit_length() - 1
    for level in range(levels.shape[0]):
        partner = from_partner(coeff, "src", top_bit - 1 - level)
        own_term = complex_apply(levels[level, 0], coeff, "bij,bjn->bin")
        other_term = complex_apply(levels[level, 1], partner, "bij,bjn->bin")
        coeff = (own_term + other_term).astype(jnp.bfloat16)
    piece = lax.all_gather(coeff, "tgt", axis=1, tiled=True)
    count = piece.shape[1] * rank
    flat = piece.reshape(2, count, columns)
    middle = complex_apply(transfer, flat, "tij,jn->tin").astype(jnp.bfloat16)
    result = complex_apply(evaluate, middle, "tij,tjn->tin")
    wide_charges = extended(charges, (("tgt", 1),), source_blocks)
    wide_xy = extended(source_xy, (("tgt", 1),), source_blocks)
    left_charges = jnp.take(wide_charges, near_list[:, 0], axis=1)
    left_xy = jnp.take(wide_xy, near_list[:, 0], axis=1)
    right_charges = jnp.take(wide_charges, near_list[:, 2] + 2 * source_blocks, axis=1)
    right_xy = jnp.take(wide_xy, near_list[:, 2] + 2 * source_blocks, axis=1)
    own_charges = jnp.take(charges, near_list[:, 1], axis=1)
    own_xy = jnp.take(source_xy, near_list[:, 1], axis=1)
    col_index = lax.axis_index("tgt")
    row_y = lax.axis_index("src").astype(jnp.float32) * BOX
    target_pos = target_xy + jnp.stack([col_index.astype(jnp.float32) * BOX, row_y])[:, None, None]
    placed = []
    for side, side_xy in enumerate((left_xy, own_xy, right_xy)):
        anchor = jnp.stack([(col_index + side - 1).astype(jnp.float32) * BOX, row_y])
        placed.append(side_xy + anchor[:, None, None])
    stacked_charges = jnp.moveaxis(jnp.stack([left_charges, own_charges, right_charges], 0), 2, 0)
    stacked_xy = jnp.moveaxis(jnp.stack(placed, 0), 2, 0)

    def near_field(inputs):
        own_pos, sources, positions = inputs
        total = kernel_term(own_pos, positions[0], sources[0])
        for side in range(1, 3):
            total = total + kernel_term(own_pos, positions[side], sources[side])
        return total

    near = lax.map(near_field, (jnp.moveaxis(target_pos, 1, 0), stacked_charges, stacked_xy))
    return result + jnp.moveaxis(near, 0, 1)


def solution(mesh):
    return jax.shard_map(
        shards,
        mesh=mesh,
        in_specs=(
            P(None, ("src", "tgt"), None, None),
            P(None, ("src", "tgt"), None),
            P(None, ("src", "tgt"), None),
            P(None, ("src", "tgt"), None, None),
            P(None, None, None, ("src", "tgt"), None, None),
            P(None, ("src", "tgt"), None, None),
            P(None, ("src", "tgt"), None, None),
            P(("src", "tgt"), None),
        ),
        out_specs=P(None, ("src", "tgt"), None, None),
        check_vma=False,
    )
```

profile of v0, /device:TPU:7, one launch (start us, length us, event | category | flops | bytes accessed | tf_op | source)
XLA Modules:
  0.0 555.3 jit_solution(16180218072759155460)
XLA Ops:
  6.5 3.4 fusion.3
  9.9 3.7 fusion.1
  13.6 0.8 fusion.61
  14.4 0.8 fusion.58
  15.3 1.7 collective-permute-start
  18.5 21.3 %collective-permute-done = bf16[2,4,128,512]{3,2,1,0:T(8,128)(2,1)S(1)} collective-permute-done((bf16[2,4,128,512]{3,2,1,0:T(8,128)(2,1)S(1)}, bf16[2,4,128,512]{3,2,1,0:T(8,128)(2,1)S(1)}, u32[]{:S(2)}, u32[]{:S(2)}) %collective-permute-start) | collective-permute-done | bytes 1048608 | tf_op jit(solution)/shard_map/ppermute | solution.py:12
  41.4 3.1 collective-permute-start.1
  45.7 20.6 %collective-permute-done.1 = bf16[2,4,128,512]{2,3,1,0:T(8,128)(2,1)S(1)} collective-permute-done((bf16[2,4,128,512]{2,3,1,0:T(8,128)(2,1)S(1)}, bf16[2,4,128,512]{2,3,1,0:T(8,128)(2,1)S(1)}, u32[]{:S(2)}, u32[]{:S(2)}) %collective-permute-start.1) | collective-permute-done | bytes 1048608 | tf_op jit(solution)/shard_map/ppermute | solution.py:12
  67.6 1.2 fusion.17
  68.8 7.3 %collective-permute-start.4 = (bf16[2,4,1024,512]{3,2,1,0:T(8,128)(2,1)}, bf16[2,4,1024,512]{3,2,1,0:T(8,128)(2,1)}, u32[]{:S(2)}, u32[]{:S(2)}) collective-permute-start(bf16[2,4,1024,512]{3,2,1,0:T(8,128)(2,1)} %param.12), channel_id=1, source_target_pairs={{0,1},{1,2},{2,3},{3,4},{4,5},{5,6},{6,7},{7,8},{8,9},{9,10},{10,1... | collective-permute-start | bytes 25165832 | tf_op jit(solution)/shard_map/ppermute | solution.py:22
  76.1 1.9 collective-permute-start.5
  78.1 5.1 collective-permute-start.2
  83.2 2.1 collective-permute-start.3
  85.4 0.7 fusion.186
  88.2 0.7 fusion.187
  88.9 1.9 fusion.42
  90.8 0.6 slice_add_fusion.1
  91.4 0.7 slice_add_fusion
  92.2 17.5 %fusion.30 = f32[1024,512]{0,1:T(8,128)S(1)} fusion(f32[1024]{0:T(1024)S(1)} %bitcast.281, f32[1024]{0:T(1024)S(1)} %bitcast.277, f32[1024]{0:T(1024)S(1)} %bitcast.297, f32[1024]{0:T(1024)S(1)} %bitcast.285, bf16[1,2,1024,512]{3,2,1,0:T(8,128)(2,1)S(1)} %get-tuple-element.71), kind=kOutput, calls=%fused_computation.57 | convolution fusion | flops 1085276160 | bytes 3162112 | tf_op jit(solution)/shard_map/while/body/eval_jaxpr/dot_general | solution.py:49
  109.7 17.5 %fusion.31 = f32[1024,512]{0,1:T(8,128)S(1)} fusion(f32[1024]{0:T(1024)S(1)} %bitcast.282, f32[1024]{0:T(1024)S(1)} %bitcast.278, f32[1024]{0:T(1024)S(1)} %bitcast.298, f32[1024]{0:T(1024)S(1)} %bitcast.286, bf16[1,2,1,1024,512]{4,3,1,2,0:T(8,128)(2,1)S(1)} %get-tuple-element.70), kind=kOutput, calls=%fused_computation.58 | convolution fusion | flops 1085276160 | bytes 3162112 | tf_op jit(solution)/shard_map/while/body/eval_jaxpr/dot_general | solution.py:46
  127.2 18.9 %add_bitcast_fusion.1 = f32[1,1,1024,512]{2,3,1,0:T(8,128)} fusion(f32[1024,512]{0,1:T(8,128)S(1)} %fusion.30, f32[1024]{0:T(1024)S(1)} %bitcast.283, f32[1024]{0:T(1024)S(1)} %bitcast.279, f32[1024]{0:T(1024)S(1)} %bitcast.299, f32[1024]{0:T(1024)S(1)} %bitcast.287, bf16[1,2,1,1024,512]{4,3,1,2,0:T(8,128)(2,1)S(1)} %get-tuple-element.70), kind=kOutput, calls=%fused_computation.47 | convolution fusion | flops 1085800448 | bytes 5259264 | tf_op jit(solution)/shard_map/while/body/eval_jaxpr/dot_general | solution.py:49
  146.1 19.5 %subtract_bitcast_fusion.1 = f32[1,1,1024,512]{2,3,1,0:T(8,128)} fusion(f32[1024,512]{0,1:T(8,128)S(1)} %fusion.31, f32[1024]{0:T(1024)S(1)} %bitcast.284, f32[1024]{0:T(1024)S(1)} %bitcast.280, f32[1024]{0:T(1024)S(1)} %bitcast.300, f32[1024]{0:T(1024)S(1)} %bitcast.288, bf16[1,2,1024,512]{3,2,1,0:T(8,128)(2,1)S(1)} %get-tuple-element.71), kind=kOutput, calls=%fused_computation.48 | convolution fusion | flops 1085800448 | bytes 5259264 | tf_op jit(solution)/shard_map/while/body/eval_jaxpr/dot_general | solution.py:46
  168.4 10.0 %collective-permute-done.2 = f32[2,4,1024]{2,1,0:T(4,128)S(1)} collective-permute-done((f32[2,4,1024]{2,1,0:T(4,128)S(1)}, f32[2,4,1024]{2,1,0:T(4,128)S(1)}, u32[]{:S(2)}, u32[]{:S(2)}) %collective-permute-start.2) | collective-permute-done | bytes 32800 | tf_op jit(solution)/shard_map/ppermute | solution.py:22
  178.3 136.2 %collective-permute-done.3 = f32[2,4,1024]{2,1,0:T(4,128)S(1)} collective-permute-done((f32[2,4,1024]{2,1,0:T(4,128)S(1)}, f32[2,4,1024]{2,1,0:T(4,128)S(1)}, u32[]{:S(2)}, u32[]{:S(2)}) %collective-permute-start.3) | collective-permute-done | bytes 32800 | tf_op jit(solution)/shard_map/ppermute | solution.py:23
  314.7 7.1 %constant_dynamic-update-slice_fusion.2 = bf16[2,12,1024,512]{3,2,1,0:T(8,128)(2,1)} fusion(bf16[2,4,1024,512]{3,2,1,0:T(8,128)(2,1)} %collective-permute-done.4), kind=kLoop, calls=%fused_computation.174 | loop fusion | bytes 16777216
  321.8 7.2 %constant_dynamic-update-slice_fusion.1 = bf16[2,12,1024,512]{3,2,1,0:T(8,128)(2,1)} fusion(bf16[2,12,1024,512]{3,2,1,0:T(8,128)(2,1)} %constant_dynamic-update-slice_fusion.2, bf16[2,4,1024,512]{3,2,1,0:T(8,128)(2,1)} %param.12), kind=kLoop, calls=%fused_computation.173 | loop fusion | bytes 16777216
  329.0 7.2 %constant_dynamic-update-slice_fusion = bf16[2,12,1024,512]{3,2,1,0:T(8,128)(2,1)} fusion(bf16[2,12,1024,512]{3,2,1,0:T(8,128)(2,1)} %constant_dynamic-update-slice_fusion.1, bf16[2,4,1024,512]{3,2,1,0:T(8,128)(2,1)} %collective-permute-done.5), kind=kLoop, calls=%fused_computation.172 | loop fusion | bytes 16777216 | tf_op jit(solution)/shard_map/concatenate | solution.py:24
  336.3 2.6 dynamic-slice_select_fusion
  338.9 17.3 %fusion.35 = f32[1024,512]{0,1:T(8,128)S(1)} fusion(f32[1024]{0:T(1024)S(1)} %bitcast.269, f32[1024]{0:T(1024)S(1)} %bitcast.273, f32[1024]{0:T(1024)S(1)} %bitcast.301, f32[1024]{0:T(1024)S(1)} %bitcast.289, bf16[1,2,1,1024,512]{4,3,1,2,0:T(8,128)(2,1)S(1)} %bitcast.257), kind=kOutput, calls=%fused_computation.62 | convolution fusion | flops 1085276160 | bytes 3162112 | tf_op jit(solution)/shard_map/while/body/eval_jaxpr/dot_general | solution.py:46
  356.2 17.9 %fusion.36 = f32[1024,512]{0,1:T(8,128)S(1)} fusion(f32[1024]{0:T(1024)S(1)} %bitcast.270, f32[1024]{0:T(1024)S(1)} %bitcast.274, f32[1024]{0:T(1024)S(1)} %bitcast.302, f32[1024]{0:T(1024)S(1)} %bitcast.290, bf16[1,2,1,1024,512]{4,3,1,2,0:T(8,128)(2,1)S(1)} %bitcast.258), kind=kOutput, calls=%fused_computation.63 | convolution fusion | flops 1085276160 | bytes 3162112 | tf_op jit(solution)/shard_map/while/body/eval_jaxpr/dot_general | solution.py:49
  374.0 17.3 %fusion.27 = f32[1024,512]{0,1:T(8,128)S(1)} fusion(f32[1024]{0:T(1024)S(1)} %bitcast.261, f32[1024]{0:T(1024)S(1)} %bitcast.303, f32[1024]{0:T(1024)S(1)} %bitcast.265, f32[1024]{0:T(1024)S(1)} %bitcast.291, bf16[1,2,1,1024,512]{4,3,1,2,0:T(8,128)(2,1)S(1)} %bitcast.255), kind=kOutput, calls=%fused_computation.54 | convolution fusion | flops 1085276160 | bytes 3162112 | tf_op jit(solution)/shard_map/while/body/eval_jaxpr/dot_general | solution.py:46
  391.3 17.9 %fusion.28 = f32[1024,512]{0,1:T(8,128)S(1)} fusion(f32[1024]{0:T(1024)S(1)} %bitcast.262, f32[1024]{0:T(1024)S(1)} %bitcast.304, f32[1024]{0:T(1024)S(1)} %bitcast.266, f32[1024]{0:T(1024)S(1)} %bitcast.292, bf16[1,2,1,1024,512]{4,3,1,2,0:T(8,128)(2,1)S(1)} %bitcast.256), kind=kOutput, calls=%fused_computation.55 | convolution fusion | flops 1085276160 | bytes 3162112 | tf_op jit(solution)/shard_map/while/body/eval_jaxpr/dot_general | solution.py:49
  409.2 17.5 %subtract_bitcast_fusion = f32[1,1,1024,512]{2,3,1,0:T(8,128)S(1)} fusion(f32[1024,512]{0,1:T(8,128)S(1)} %fusion.35, f32[1024]{0:T(1024)S(1)} %bitcast.271, f32[1024]{0:T(1024)S(1)} %bitcast.275, f32[1024]{0:T(1024)S(1)} %bitcast.305, f32[1024]{0:T(1024)S(1)} %bitcast.293, bf16[2,1,1024,512]{3,2,1,0:T(8,128)(2,1)S(1)} %get-tuple-element.66), kind=kOutput, calls=%fused_computation.46 | convolution fusion | flops 1085800448 | bytes 5259264 | tf_op jit(solution)/shard_map/while/body/eval_jaxpr/dot_general | solution.py:46
  426.7 19.2 %add_bitcast_fusion = f32[1,1,1024,512]{2,3,1,0:T(8,128)} fusion(f32[1024,512]{0,1:T(8,128)S(1)} %fusion.36, f32[1024]{0:T(1024)S(1)} %bitcast.272, f32[1024]{0:T(1024)S(1)} %bitcast.276, f32[1024]{0:T(1024)S(1)} %bitcast.306, f32[1024]{0:T(1024)S(1)} %bitcast.294, bf16[2,1,1024,512]{3,2,1,0:T(8,128)(2,1)S(1)} %get-tuple-element.66), kind=kOutput, calls=%fused_computation.45 | convolution fusion | flops 1085800448 | bytes 5259264 | tf_op jit(solution)/shard_map/while/body/eval_jaxpr/dot_general | solution.py:49
  446.0 19.1 %subtract_bitcast_fusion.2 = f32[1,1,1024,512]{2,3,1,0:T(8,128)} fusion(f32[1024,512]{0,1:T(8,128)S(1)} %fusion.27, f32[1024]{0:T(1024)S(1)} %bitcast.263, f32[1024]{0:T(1024)S(1)} %bitcast.307, f32[1024]{0:T(1024)S(1)} %bitcast.267, f32[1024]{0:T(1024)S(1)} %bitcast.295, bf16[2,1,1024,512]{3,2,1,0:T(8,128)(2,1)S(1)} %get-tuple-element.67), kind=kOutput, calls=%fused_computation.50 | convolution fusion | flops 1085800448 | bytes 5259264 | tf_op jit(solution)/shard_map/while/body/eval_jaxpr/dot_general | solution.py:46
  465.1 19.0 %add_bitcast_fusion.2 = f32[1,1,1024,512]{2,3,1,0:T(8,128)} fusion(f32[1024,512]{0,1:T(8,128)S(1)} %fusion.28, f32[1024]{0:T(1024)S(1)} %bitcast.264, f32[1024]{0:T(1024)S(1)} %bitcast.308, f32[1024]{0:T(1024)S(1)} %bitcast.268, f32[1024]{0:T(1024)S(1)} %bitcast.296, bf16[2,1,1024,512]{3,2,1,0:T(8,128)(2,1)S(1)} %get-tuple-element.67), kind=kOutput, calls=%fused_computation.49 | convolution fusion | flops 1085800448 | bytes 5259264 | tf_op jit(solution)/shard_map/while/body/eval_jaxpr/dot_general | solution.py:49
  484.0 11.8 %fusion.184 = (bf16[1,64,128,512]{2,3,1,0:T(8,128)(2,1)}, bf16[1,64,128,512]{2,3,1,0:T(8,128)(2,1)}) fusion(bf16[2,64,128,512]{2,3,1,0:T(8,128)(2,1)} %all-gather.2.cloned.1.call-done), kind=kLoop, calls=%fused_computation.229 | loop fusion | bytes 33554432 | tf_op jit(solution)/shard_map/slice | solution.py:31
  495.8 11.9 %copy.39 = bf16[1,64,128,512]{3,2,1,0:T(8,128)(2,1)} copy(bf16[1,64,128,512]{2,3,1,0:T(8,128)(2,1)} %get-tuple-element.68) | data formatting | bytes 16777216 | tf_op jit(solution)/shard_map/slice | solution.py:31
  507.7 12.2 %copy.38 = bf16[1,64,128,512]{3,2,1,0:T(8,128)(2,1)} copy(bf16[1,64,128,512]{2,3,1,0:T(8,128)(2,1)} %get-tuple-element.69) | data formatting | bytes 16777216 | tf_op jit(solution)/shard_map/slice | solution.py:30
  520.0 6.5 %fusion.20 = f32[512,128]{1,0:T(8,128)S(1)} fusion(bf16[8192,512]{1,0:T(8,128)(2,1)} %bitcast.247, bf16[2,1,128,8192]{3,2,1,0:T(8,128)(2,1)} %param.17), kind=kOutput, calls=%fused_computation.36 | convolution fusion | flops 1073741824 | bytes 10747904 | tf_op jit(solution)/shard_map/tij,jn->tin/dot_general | solution.py:31
  526.5 1.0 copy-done.12
  527.5 2.4 fusion.18
  529.9 2.4 fusion.67
  532.4 2.4 fusion.73
  536.8 0.7 copy-done.3
  537.6 0.6 copy-done.4
  539.4 3.3 maximum_add_fusion
  542.7 5.4 copy.52
  (69 shorter events, 9.2 us)
Async XLA Ops:
  6.5 3.4 copy-start.13
  6.5 477.5 %all-gather.2.cloned.1.call-start = ((), (), s32[]{:S(2)}) async-start(), calls=%async_computation | async-start | bytes 17825792 | tf_op jit(solution)/shard_map/all_gather | solution.py:66
  6.5 7.1 %copy-start = (bf16[2,4,1024,512]{3,2,1,0:T(8,128)(2,1)S(1)}, bf16[2,4,1024,512]{3,2,1,0:T(8,128)(2,1)}, u32[]{:S(2)}) copy-start(bf16[2,4,1024,512]{3,2,1,0:T(8,128)(2,1)} %param.12) | copy-start | bytes 25165828
  14.4 2.6 copy-start.2
  15.3 24.5 %collective-permute-start = (bf16[2,4,128,512]{3,2,1,0:T(8,128)(2,1)S(1)}, bf16[2,4,128,512]{3,2,1,0:T(8,128)(2,1)S(1)}, u32[]{:S(2)}, u32[]{:S(2)}) collective-permute-start(bf16[2,4,128,512]{3,2,1,0:T(8,128)(2,1)S(1)} %pad_maximum_fusion), channel_id=1, source_target_pairs={{0,64},{16,80},{32,96},{48,112},{64,0},{80,16},{96,32},{112,48},{1... | collective-permute-start | bytes 3145736 | tf_op jit(solution)/shard_map/ppermute | solution.py:12
  41.4 24.9 %collective-permute-start.1 = (bf16[2,4,128,512]{2,3,1,0:T(8,128)(2,1)S(1)}, bf16[2,4,128,512]{2,3,1,0:T(8,128)(2,1)S(1)}, u32[]{:S(2)}, u32[]{:S(2)}) collective-permute-start(bf16[2,4,128,512]{2,3,1,0:T(8,128)(2,1)S(1)} %fusion.16), channel_id=1, source_target_pairs={{0,32},{16,48},{32,0},{48,16},{64,96},{80,112},{96,64},{112,80},{1... | collective-permute-start | bytes 3145736 | tf_op jit(solution)/shard_map/ppermute | solution.py:12
  67.3 10.8 %copy-start.9 = (f32[2,4,1024]{2,1,0:T(4,128)S(1)}, f32[2,4,1024]{2,1,0:T(4,128)}, u32[]{:S(2)}) copy-start(f32[2,4,1024]{2,1,0:T(4,128)} %param.13) | copy-start | bytes 98308
  67.3 18.1 %copy-start.11 = (s32[1,3]{1,0:T(1,128)S(1)}, s32[1,3]{1,0:T(1,128)}, u32[]{:S(2)}) copy-start(s32[1,3]{1,0:T(1,128)} %param.19) | copy-start | bytes 40
  68.8 23.3 %copy-start.10 = (f32[2,1,1024]{2,1,0:T(1,128)S(1)}, f32[2,1,1024]{2,1,0:T(1,128)}, u32[]{:S(2)}) copy-start(f32[2,1,1024]{2,1,0:T(1,128)} %param.14) | copy-start | bytes 24580
  68.8 245.9 %collective-permute-start.4 = (bf16[2,4,1024,512]{3,2,1,0:T(8,128)(2,1)}, bf16[2,4,1024,512]{3,2,1,0:T(8,128)(2,1)}, u32[]{:S(2)}, u32[]{:S(2)}) collective-permute-start(bf16[2,4,1024,512]{3,2,1,0:T(8,128)(2,1)} %param.12), channel_id=1, source_target_pairs={{0,1},{1,2},{2,3},{3,4},{4,5},{5,6},{6,7},{7,8},{8,9},{9,10},{10,1... | collective-permute-start | bytes 25165832 | tf_op jit(solution)/shard_map/ppermute | solution.py:22
  76.1 252.9 %collective-permute-start.5 = (bf16[2,4,1024,512]{3,2,1,0:T(8,128)(2,1)}, bf16[2,4,1024,512]{3,2,1,0:T(8,128)(2,1)}, u32[]{:S(2)}, u32[]{:S(2)}) collective-permute-start(bf16[2,4,1024,512]{3,2,1,0:T(8,128)(2,1)} %param.12), channel_id=1, source_target_pairs={{1,0},{2,1},{3,2},{4,3},{5,4},{6,5},{7,6},{8,7},{9,8},{10,9},{11,1... | collective-permute-start | bytes 25165832 | tf_op jit(solution)/shard_map/ppermute | solution.py:23
  78.1 100.2 %collective-permute-start.2 = (f32[2,4,1024]{2,1,0:T(4,128)S(1)}, f32[2,4,1024]{2,1,0:T(4,128)S(1)}, u32[]{:S(2)}, u32[]{:S(2)}) collective-permute-start(f32[2,4,1024]{2,1,0:T(4,128)S(1)} %copy-done.9), channel_id=1, source_target_pairs={{0,1},{1,2},{2,3},{3,4},{4,5},{5,6},{6,7},{7,8},{8,9},{9,10},{10,1... | collective-permute-start | bytes 98312 | tf_op jit(solution)/shard_map/ppermute | solution.py:22
  83.2 231.3 %collective-permute-start.3 = (f32[2,4,1024]{2,1,0:T(4,128)S(1)}, f32[2,4,1024]{2,1,0:T(4,128)S(1)}, u32[]{:S(2)}, u32[]{:S(2)}) collective-permute-start(f32[2,4,1024]{2,1,0:T(4,128)S(1)} %copy-done.9), channel_id=1, source_target_pairs={{1,0},{2,1},{3,2},{4,3},{5,4},{6,5},{7,6},{8,7},{9,8},{10,9},{11,1... | collective-permute-start | bytes 98312 | tf_op jit(solution)/shard_map/ppermute | solution.py:23
  519.9 6.5 %copy-start.1 = (bf16[1,64,128,512]{3,2,1,0:T(8,128)(2,1)S(1)}, bf16[1,64,128,512]{3,2,1,0:T(8,128)(2,1)}, u32[]{:S(2)}) copy-start(bf16[1,64,128,512]{3,2,1,0:T(8,128)(2,1)} %copy.38) | copy-start | bytes 25165828
  520.0 7.6 %copy-start.12 = (bf16[2,1,128,8192]{3,2,1,0:T(8,128)(2,1)S(1)}, bf16[2,1,128,8192]{3,2,1,0:T(8,128)(2,1)}, u32[]{:S(2)}) copy-start(bf16[2,1,128,8192]{3,2,1,0:T(8,128)(2,1)} %param.17) | copy-start | bytes 12582916
  520.0 12.4 %slice-start = ((s8[8388608]{0:T(1024)(128)(4,1)}), s8[4194304]{0:T(1024)(128)(4,1)S(1)}, s32[]{:S(2)}) async-start(s8[8388608]{0:T(1024)(128)(4,1)} %bitcast.248), calls=%async_computation.1 | async-start | bytes 8388608
  527.5 4.9 slice-start.1
  532.4 2.4 copy-start.8
  535.2 1.6 copy-start.7
  535.7 1.9 copy-start.3
  535.7 2.5 copy-start.4
  535.7 3.1 copy-start.5
  535.7 3.7 copy-start.6
Sparse Core Ops, SparseCore 0:
  68.9 227.4 all-gather.1
where the time goes:
time: 563 us; the launch traced here: 555 us
  matrix products  248 us (44%)
  waiting for transfers between devices  188 us (33%)
  local copies, waits for them, and re-layouts  68 us (12%)
  starting transfers between devices  21.3 us (4%)
  between operations  19.2 us (3%)
  other arithmetic  11 us (2%)
    ppermute x2, waiting for transfers between devices, extended(): after = lax.ppermute(first, axis, down)  136 us
    dot_general x3, matrix products, kernel_term(): jnp.dot(sine, strengths[1], preferred_element_type=jnp.float32)  56.1 us
    dot_general x3, matrix products, kernel_term(): jnp.dot(cosine, strengths[1], preferred_element_type=jnp.float32)  55.7 us
    dot_general x3, matrix products, kernel_term(): jnp.dot(sine, strengths[0], preferred_element_type=jnp.float32)  54.7 us
    dot_general x3, matrix products, kernel_term(): jnp.dot(cosine, strengths[0], preferred_element_type=jnp.float32)  52.1 us
    ppermute x2, waiting for transfers between devices, from_partner(): lax.ppermute(array, axis, [(i, i ^ 1 << apart) for i in range(lax.axis_si...  41.9 us
    slice x2, local copies, waits for them, and re-layouts, complex_apply(): vector[1]  23.7 us
    unnamed x34, local copies, waits for them, and re-layouts  18.2 us
  transfers between devices with their start and end apart: 7, of which 4 were waited for; matrix products, arithmetic and copies ran while one was open for 45% of the time, Pallas kernels for 0%

commit v1 on v0

v1 whole, which is shorter than its diff:
```python
import functools
import math

import jax
import jax.numpy as jnp
from jax import lax
from jax.experimental import pallas as pl
from jax.experimental.pallas import tpu as pltpu
from jax.sharding import PartitionSpec as P

KAPPA = 73.27
CORE = 0.5
BOX = 8.0
MESH = pl.DeviceIdType.MESH
F32, BF16 = jnp.float32, jnp.bfloat16

PTS, R, NR, SBLK = 1024, 128, 512, 4
NC = 4
CW = NR // NC
ROWS = 128
PIECE = 256
NP = PTS // PIECE
COS = (0.99999922, -19.73898252, 64.92872657, -85.2723964, 58.79403555, -21.07677646)
SIN = (6.2830558, -41.33121426, 81.36681443, -74.47799927, 32.78139018)


def horner(coefs, u):
    out = coefs[-1]
    for c in coefs[-2::-1]:
        out = out * u + c
    return out


def cmul(top, bottom, x):
    d = jnp.dot(jnp.concatenate([top, bottom], 0), x, preferred_element_type=F32)
    m, n = top.shape[0], x.shape[1] // 2
    return d[:m, :n] - d[m:, n:], d[:m, n:] + d[m:, :n]


def lanes(k):
    if isinstance(k, int):
        return pl.ds(k * CW, CW)
    return pl.ds(pl.multiple_of(k * CW, CW), CW)


def rows_at(i, n):
    if isinstance(i, int):
        return pl.ds(i * n, n)
    return pl.ds(pl.multiple_of(i * n, n), n)


def gen_tile(txy, src, scale, row0, cos_ref, sin_ref, at):
    wide = 256

    def group(i, _):
        r = pl.ds(pl.multiple_of(row0 + i * 16, 16), 16)
        o = pl.ds(pl.multiple_of(at + i * 16, 16), 16)
        tx, ty = txy[r, 0:1], txy[r, 1:2]
        for j in range(PTS // wide):
            c = slice(j * wide, (j + 1) * wide)
            dx = tx - src[0:1, c]
            dy = ty - src[1:2, c]
            r2 = dx * dx + (dy * dy + CORE * CORE)
            inv = lax.rsqrt(r2)
            inv = inv * (1.5 - (0.5 * r2) * (inv * inv))
            turns = (r2 * inv) * (KAPPA / (2.0 * math.pi))
            f = turns - jnp.round(turns)
            u = f * f
            amp = inv * scale
            cos_ref[o, c] = (horner(COS, u) * amp).astype(BF16)
            sin_ref[o, c] = (horner(SIN, u) * (f * amp)).astype(BF16)
        return 0

    lax.fori_loop(0, ROWS // 16, group, 0)


def main_kernel(
    nlv, nls, sxy, txy, charges, anterp, levels, transfer, near_out, mid_out,
    ch, an, lv, w, v, g, ps, pr, ns, nr, sxs, sxr, sxo, nlr, nlm, tc, ts, toc, tos, acc,
    ld, lvs, nl_s, nl_r, nm_s, xs_s, xs_r, w_s, w_r, l_s, l_r, g_s, g_r, p_s, p_r, n_s, n_r, o_s,
):
    s, t = lax.axis_index("src"), lax.axis_index("tgt")
    n_src = 8
    c = t % 2
    hi = (t // 2) % 2
    x = t // 4
    sib = t + 1 - 2 * c
    far = (t + 15 + 2 * c) % 16
    def at(src, tgt):
        return {"src": src, "tgt": tgt}
    level_dev = [at((s + n_src // 2) % n_src, t), at(s // 4 * 4 + (s + 2) % 4, t)]
    z_dev = at(s, x * 4 + (1 - hi) * 2 + c)

    def x_dev(d, e):
        core = c if e == 0 else 1 - c
        return at(s, ((x + d) % 4) * 4 + hi * 2 + core)

    others = [(d, e) for d in (1, 3, 2, 0) for e in (0, 1) if (d, e) != (0, 0)]
    pending = []

    def remote(src, dst, ss, rs, dev):
        cp = pltpu.make_async_remote_copy(src, dst, ss, rs, device_id=dev, device_id_type=MESH)
        pending.append(cp)
        cp.start()
        return cp

    loads = []
    for b in range(SBLK):
        loads.append(pltpu.make_async_copy(charges.at[:, b], ch.at[:, b], ld.at[0, b]))
        loads.append(pltpu.make_async_copy(anterp.at[:, b], an.at[:, b], ld.at[1, b]))
    for cp in loads:
        cp.start()
    lv_loads = [
        pltpu.make_async_copy(levels.at[l, o], lv.at[l, :, :, :, pl.ds(o * R, R)], lvs.at[l, o])
        for l in range(2) for o in range(2)
    ]
    for cp in lv_loads:
        cp.start()

    greet = [x_dev(d, e) for d, e in others] + level_dev + [z_dev, at(s, far)]
    barrier = pltpu.get_barrier_semaphore()
    for dev in greet:
        pl.semaphore_signal(barrier, 1, device_id=dev, device_id_type=MESH)
    pl.semaphore_wait(barrier, len(greet))

    near_dev = [at(s, sib), at(s, far)]
    nl_cp = [remote(nlv.at[i], nlr.at[i], nl_s.at[i], nl_r.at[i], near_dev[i]) for i in range(2)]

    w_cp = {}
    own_w = []
    for h in range(2):
        col = (x * 4 + h * 2 + c) * (SBLK * R)
        own_w.append(pltpu.make_async_copy(
            transfer.at[:, 0, :, pl.ds(pl.multiple_of(col, SBLK * R), SBLK * R)],
            w.at[0, :, :, pl.ds(h * SBLK * R, SBLK * R)], w_s.at[0, h]))
        own_w[-1].start()

    def send_w(d, e):
        core = c if e == 0 else 1 - c
        slot = ((-d) % 4) * 2 + e
        for h in range(2):
            col = (((x + d) % 4) * 4 + h * 2 + core) * (SBLK * R)
            w_cp[slot, h] = remote(
                transfer.at[:, 0, :, pl.ds(pl.multiple_of(col, SBLK * R), SBLK * R)],
                w.at[slot, :, :, pl.ds(h * SBLK * R, SBLK * R)],
                w_s.at[slot, h], w_r.at[slot, h], x_dev(d, e))

    for d, e in others:
        send_w(d, e)

    for cp in loads:
        cp.wait()
    l_cp = {}

    def send_level(l, k):
        l_cp[l, k] = remote(
            v.at[l, k, :, pl.ds(0, R), :], v.at[l, k, :, pl.ds(R, R), :], l_s.at[l, k], l_r.at[l, k], level_dev[l])

    for k in range(NC):
        def block(b, _, k=k):
            xk = jnp.concatenate([ch[0, b, :, lanes(k)], ch[1, b, :, lanes(k)]], 1)
            re, im = cmul(an[0, b], an[1, b], xk)
            v[0, k, b, pl.ds(0, R), :] = jnp.concatenate([re, im], 1).astype(BF16)
            return 0
        lax.fori_loop(0, SBLK, block, 0)
        send_level(0, k)

    nm = []
    for i in range(2):
        nl_cp[i].wait_recv()
        nm.append(pltpu.make_async_copy(nlr.at[i], nlm.at[i], nm_s.at[i]))
        nm[i].start()
    xs_cp, n_cp = [], {}

    def pick(i):
        nm[i].wait()
        index = nlm[i, 0, 0]
        sxs[i] = sxy[index]

        def some(j, _):
            r = rows_at(j, 64)
            for q in range(2):
                ns[i, q, r, :] = ch[q, index, r, :]
            return 0

        lax.fori_loop(0, PTS // 64, some, 0)
        xs_cp.append(remote(sxs.at[i], sxr.at[i], xs_s.at[i], xs_r.at[i], near_dev[i]))

    def send_near(i, p):
        r = pl.ds(p * PIECE, PIECE)
        n_cp[i, p] = remote(ns.at[i, :, r, :], nr.at[i, :, r, :], n_s.at[i, p], n_r.at[i, p], near_dev[i])

    pick(1)
    send_near(1, 0)
    send_near(1, 1)
    pick(0)
    for p in range(NP):
        send_near(0, p)

    own = nls[0]
    amp = 1.0 / (4.0 * math.pi)
    sxo[...] = sxy[own]

    def own_rows(i):
        gen_tile(txy, sxo, amp, i * ROWS, toc, tos, 0)
        r = rows_at(i, ROWS)

        def chunk(k, _):
            xk = jnp.concatenate([ch[0, own, :, lanes(k)], ch[1, own, :, lanes(k)]], 1)
            re, im = cmul(toc[...], tos[...], xk)
            acc[0, r, lanes(k)] = re
            acc[1, r, lanes(k)] = im
            return 0

        lax.fori_loop(0, NC, chunk, 0)

    def level_step(l, k):
        l_cp[l, k].wait_recv()

        def block(b, _):
            re, im = cmul(lv[l, 0, b], lv[l, 1, b], v[l, k, b])
            out = jnp.concatenate([re, im], 1).astype(BF16)
            if l == 0:
                v[1, k, b, pl.ds(0, R), :] = out
            else:
                g[k, hi, rows_at(b, R), :] = out
            return 0

        lax.fori_loop(0, SBLK, block, 0)

    g_cp = {}
    for cp in lv_loads:
        cp.wait()
    for k in range(NC):
        own_rows(k)
        level_step(0, k)
        send_level(1, k)
    send_near(1, 2)
    for k in range(NC):
        own_rows(NC + k)
        level_step(1, k)
        g_cp[k] = remote(g.at[k, hi], g.at[k, hi], g_s.at[k], g_r.at[k], z_dev)
    send_near(1, 3)

    sib_off = BOX * (1 - 2 * c).astype(F32)
    far_amp = jnp.where((t == 0) | (t == 15), 0.0, amp)

    def side_tiles(i, first, count):
        def step(j, _):
            gen_tile(txy, sxr.at[i], amp if i == 0 else far_amp, (first + j) * ROWS, tc.at[i], ts.at[i], (first + j) * ROWS)
            return 0
        lax.fori_loop(0, count, step, 0)

    def side_part(i, p, out=False):
        cols = pl.ds(p * PIECE, PIECE)

        def row_step(j, _):
            r = rows_at(j, ROWS)

            def chunk(k, _):
                xk = jnp.concatenate([nr[i, 0, cols, lanes(k)], nr[i, 1, cols, lanes(k)]], 1)
                re, im = cmul(tc[i, r, cols], ts[i, r, cols], xk)
                acc[0, r, lanes(k)] += re
                acc[1, r, lanes(k)] += im
                return 0

            lax.fori_loop(0, NC, chunk, 0)
            return 0

        lax.fori_loop(0, PTS // ROWS, row_step, 0)

    for i in range(2):
        xs_cp[1 - i].wait_recv()
        sxr[i] = sxr[i] + jnp.where(lax.broadcasted_iota(jnp.int32, (2, PTS), 0) == 0, sib_off if i == 0 else -sib_off, 0.0)

    p_cp = {}

    def partial_step(k):
        g_cp[k].wait_recv()
        gk = g.at[k]

        def one(slot, _):
            xk = jnp.concatenate([gk[0], gk[1]], 0)
            re, im = cmul(w[slot, 0], w[slot, 1], xk)
            ps[k, slot] = jnp.concatenate([re, im], 1).astype(BF16)
            return 0

        lax.fori_loop(0, 8, one, 0)
        for d, e in others:
            slot = d * 2 + e
            back = ((-d) % 4) * 2 + e
            p_cp[k, back] = remote(ps.at[k, slot], pr.at[k, back], p_s.at[k, slot], p_r.at[k, back], x_dev(d, e))

    def middle_step(k):
        total = ps[k, 0].astype(F32)
        for d, e in others:
            back = d * 2 + e
            p_cp[k, back].wait_recv()
            total = total + pr[k, back].astype(F32)
        mid_out[k] = total.astype(BF16)

    side_tiles(0, 0, 8)
    for p in range(NP):
        n_cp[0, p].wait_recv()
        side_part(0, p)
    for cp in own_w:
        cp.wait()
    for cp in w_cp.values():
        cp.wait_recv()
    for k in range(NC):
        side_tiles(1, 2 * k, 2)
        partial_step(k)
    for k in range(NC):
        middle_step(k)
        n_cp[1, k].wait_recv()
        side_part(1, k)
    outs = pltpu.make_async_copy(acc, near_out, o_s)
    outs.start()
    outs.wait()
    for cp in pending:
        cp.wait_send()


def finish_kernel(near, evaluate, mid, out):
    er, ei = evaluate[0, 0], evaluate[1, 0]
    for k in range(NC):
        re, im = cmul(er, ei, mid[k])
        out[0, 0, :, k * CW:(k + 1) * CW] = near[0, :, k * CW:(k + 1) * CW] + re
        out[1, 0, :, k * CW:(k + 1) * CW] = near[1, :, k * CW:(k + 1) * CW] + im


def shards(charges, source_xy, target_xy, anterp, levels, transfer, evaluate, near_list):
    odd = lax.axis_index("tgt") % 2
    left, own, right = near_list[0, 0], near_list[0, 1], near_list[0, 2]
    to_sib = jnp.where(odd == 1, left, right)
    to_far = jnp.where(odd == 1, right, left)
    nlv = jnp.broadcast_to(jnp.stack([to_sib, to_far])[:, None, None], (2, 8, 128))
    nls = own[None]
    sxy = jnp.moveaxis(source_xy, 1, 0)
    txy = target_xy[:, 0, :].T
    vmem = pl.BlockSpec(memory_space=pltpu.VMEM)
    hbm = pl.BlockSpec(memory_space=pl.ANY)
    dma = pltpu.SemaphoreType.DMA
    near, mid = pl.pallas_call(
        main_kernel,
        out_shape=(
            jax.ShapeDtypeStruct((2, PTS, NR), F32),
            jax.ShapeDtypeStruct((NC, R, 2 * CW), BF16),
        ),
        in_specs=[vmem, pl.BlockSpec(memory_space=pltpu.SMEM), vmem, vmem, hbm, hbm, hbm, hbm],
        out_specs=(hbm, vmem),
        scratch_shapes=[
            pltpu.VMEM((2, SBLK, PTS, NR), BF16),
            pltpu.VMEM((2, SBLK, R, PTS), BF16),
            pltpu.VMEM((2, 2, SBLK, R, 2 * R), BF16),
            pltpu.VMEM((8, 2, R, 2 * SBLK * R), BF16),
            pltpu.VMEM((2, NC, SBLK, 2 * R, 2 * CW), BF16),
            pltpu.VMEM((NC, 2, SBLK * R, 2 * CW), BF16),
            pltpu.VMEM((NC, 8, R, 2 * CW), BF16),
            pltpu.VMEM((NC, 8, R, 2 * CW), BF16),
            pltpu.VMEM((2, 2, PTS, NR), BF16),
            pltpu.VMEM((2, 2, PTS, NR), BF16),
            pltpu.VMEM((2, 2, PTS), F32),
            pltpu.VMEM((2, 2, PTS), F32),
            pltpu.VMEM((2, PTS), F32),
            pltpu.VMEM((2, 8, 128), jnp.int32),
            pltpu.SMEM((2, 8, 128), jnp.int32),
            pltpu.VMEM((2, PTS, PTS), BF16),
            pltpu.VMEM((2, PTS, PTS), BF16),
            pltpu.VMEM((ROWS, PTS), BF16),
            pltpu.VMEM((ROWS, PTS), BF16),
            pltpu.VMEM((2, PTS, NR), F32),
            dma((2, SBLK)), dma((2, 2)), dma((2,)), dma((2,)), dma((2,)), dma((2,)), dma((2,)),
            dma((8, 2)), dma((8, 2)), dma((2, NC)), dma((2, NC)), dma((NC,)), dma((NC,)),
            dma((NC, 8)), dma((NC, 8)), dma((2, NP)), dma((2, NP)), dma,
        ],
        compiler_params=pltpu.CompilerParams(
            collective_id=0, has_side_effects=True, vmem_limit_bytes=60 * 2**20),
        name="exchange_and_near",
    )(nlv, nls, sxy, txy, charges, anterp, levels, transfer)
    rows = 256
    return pl.pallas_call(
        finish_kernel,
        grid=(PTS // rows,),
        out_shape=jax.ShapeDtypeStruct((2, 1, PTS, NR), F32),
        in_specs=[
            pl.BlockSpec((2, rows, NR), lambda i: (0, i, 0)),
            pl.BlockSpec((2, 1, rows, R), lambda i: (0, 0, i, 0)),
            pl.BlockSpec((NC, R, 2 * CW), lambda i: (0, 0, 0)),
        ],
        out_specs=pl.BlockSpec((2, 1, rows, NR), lambda i: (0, 0, i, 0)),
        name="evaluate_and_add",
    )(near, evaluate, mid)


def solution(mesh):
    return jax.shard_map(
        shards,
        mesh=mesh,
        in_specs=(
            P(None, ("src", "tgt"), None, None),
            P(None, ("src", "tgt"), None),
            P(None, ("src", "tgt"), None),
            P(None, ("src", "tgt"), None, None),
            P(None, None, None, ("src", "tgt"), None, None),
            P(None, ("src", "tgt"), None, None),
            P(None, ("src", "tgt"), None, None),
            P(("src", "tgt"), None),
        ),
        out_specs=P(None, ("src", "tgt"), None, None),
        check_vma=False,
    )
```

time: 563 us -> 154 us (0.27)
  the two profiles are of different devices: /device:TPU:7 before, /device:TPU:18 now
where the time goes in v1:
time: 154 us
  Pallas kernels  146 us (95%)
  local copies, waits for them, and re-layouts  5.18 us (3%)
  between operations  2.58 us (2%)
    pallas_call x1, Pallas kernels, shards(): pl.pallas_call(main_kernel, out_shape=(jax.ShapeDtypeStruct((2, PTS, NR),...  140 us
    pallas_call x1, Pallas kernels, shards(): pl.pallas_call(finish_kernel, grid=(PTS // rows,), out_shape=jax.ShapeDty...  5.59 us
    unnamed x2, local copies, waits for them, and re-layouts  3.1 us

profile of v1, /device:TPU:18, one launch (start us, length us, event | category | flops | bytes accessed | tf_op | source)
XLA Modules:
  0.0 153.5 jit_solution(15509973973249665240)
XLA Ops:
  0.0 1.4 fusion
  4.0 0.1 pad_add_fusion
  4.1 0.7 broadcast_in_dim.2.nlv
  4.7 1.4 copy.12
  6.1 1.7 %copy.10 = f32[2,1,1024]{0,2,1:T(8,128)} copy(f32[2,1,1024]{2,1,0:T(1,128)} %param.10) | data formatting | bytes 16384 | tf_op args[2]
  7.8 140.1 %exchange_and_near.1 = (f32[2,1024,512]{2,1,0:T(8,128)}, bf16[4,128,256]{2,1,0:T(8,128)(2,1)}) custom-call(s32[2,8,128]{2,1,0:T(8,128)} %broadcast_in_dim.2.nlv, s32[1]{0:T(128)} %bitcast.4.nls, f32[4,2,1024]{2,1,0:T(2,128)} %bitcast.12, f32[1024,2]{1,0:T(8,128)} %bitcast.11, bf16[2,4,1024,512]{3,2,1,0:T(8,128)(2,1)} %charges.1, ...), custom_call_target="tpu_custom_call" | custom-call | tf_op jit(solution)/shard_map/exchange_and_near/pallas_call | solution.py:344
  148.0 5.6 %evaluate_and_add.1 = f32[2,1,1024,512]{3,2,1,0:T(8,128)} custom-call(f32[2,1024,512]{2,1,0:T(8,128)} %get-tuple-element.7.near, bf16[2,1,1024,128]{3,2,1,0:T(8,128)(2,1)} %evaluate.1, bf16[4,128,256]{2,1,0:T(8,128)(2,1)} %get-tuple-element.8.mid), custom_call_target="tpu_custom_call" | custom-call | tf_op jit(solution)/shard_map/evaluate_and_add/pallas_call | solution.py:382

commit v2 on v1

v2 whole, which is shorter than its diff:
```python
import functools
import math

import jax
import jax.numpy as jnp
from jax import lax
from jax.experimental import pallas as pl
from jax.experimental.pallas import tpu as pltpu
from jax.sharding import PartitionSpec as P

KAPPA = 73.27
CORE = 0.5
BOX = 8.0
MESH = pl.DeviceIdType.MESH
F32, BF16 = jnp.float32, jnp.bfloat16

PTS, R, NR, SBLK = 1024, 128, 512, 4
KB = SBLK * R
NC = 2
CW = NR // NC
ROWS = 128
PIECE = 256
NP = PTS // PIECE
COS = (0.99999922, -19.73898252, 64.92872657, -85.2723964, 58.79403555, -21.07677646)
SIN = (6.2830558, -41.33121426, 81.36681443, -74.47799927, 32.78139018)


def horner(coefs, u):
    out = coefs[-1]
    for c in coefs[-2::-1]:
        out = out * u + c
    return out


def cdot(ar, ai, xr, xi):
    dot = functools.partial(jnp.dot, preferred_element_type=F32)
    return dot(ar, xr) - dot(ai, xi), dot(ar, xi) + dot(ai, xr)


def rows_at(i, n):
    if isinstance(i, int):
        return pl.ds(i * n, n)
    return pl.ds(pl.multiple_of(i * n, n), n)


def gen_tile(txy, src, scale, row0, cos_ref, sin_ref, at):
    wide = 256

    def group(i, _):
        r = pl.ds(pl.multiple_of(row0 + i * 16, 16), 16)
        o = pl.ds(pl.multiple_of(at + i * 16, 16), 16)
        tx, ty = txy[r, 0:1], txy[r, 1:2]
        for j in range(PTS // wide):
            c = slice(j * wide, (j + 1) * wide)
            dx = tx - src[0:1, c]
            dy = ty - src[1:2, c]
            r2 = dx * dx + (dy * dy + CORE * CORE)
            inv = lax.rsqrt(r2)
            inv = inv * (1.5 - (0.5 * r2) * (inv * inv))
            turns = (r2 * inv) * (KAPPA / (2.0 * math.pi))
            f = turns - jnp.round(turns)
            u = f * f
            amp = inv * scale
            cos_ref[o, c] = (horner(COS, u) * amp).astype(BF16)
            sin_ref[o, c] = (horner(SIN, u) * (f * amp)).astype(BF16)
        return 0

    lax.fori_loop(0, ROWS // 16, group, 0)


def main_kernel(
    near, sxy, txy, charges, anterp, levels, transfer, evaluate, out,
    ch, an, lv, w, v, g, ps, pr, mid, ev, ns, nr, nlv, nlr, nlm, sxs, sxr, txt, tc, ts, acc,
    ld, lvs, evs, nl_s, nl_r, nm_s, xs_s, xs_r, w_s, w_r, l_s, l_r, g_s, g_r, p_s, p_r, n_s, n_r, o_s,
):
    s, t = lax.axis_index("src"), lax.axis_index("tgt")
    n_src = 8
    c = t % 2
    hi = (t // 2) % 2
    x = t // 4

    def at(src, tgt):
        return {"src": src, "tgt": tgt}

    near_dev = [at(s, t + 1 - 2 * c), at(s, (t + 15 + 2 * c) % 16)]
    level_dev = [at((s + n_src // 2) % n_src, t), at(s // 4 * 4 + (s + 2) % 4, t)]
    z_dev = at(s, x * 4 + (1 - hi) * 2 + c)

    def x_dev(d, e):
        core = c if e == 0 else 1 - c
        return at(s, ((x + d) % 4) * 4 + hi * 2 + core)

    others = [(d, e) for d in (1, 3, 2, 0) for e in (0, 1) if (d, e) != (0, 0)]
    pending = []

    def remote(src, dst, ss, rs, dev):
        cp = pltpu.make_async_remote_copy(src, dst, ss, rs, device_id=dev, device_id_type=MESH)
        pending.append(cp)
        cp.start()
        return cp

    loads = []
    for b in range(SBLK):
        loads.append((
            pltpu.make_async_copy(anterp.at[:, b], an.at[:, b], ld.at[1, b]),
            pltpu.make_async_copy(charges.at[:, b], ch.at[:, b], ld.at[0, b])))
        for cp in loads[b]:
            cp.start()
    lv_loads = [
        pltpu.make_async_copy(levels.at[l, o], lv.at[l, :, :, :, pl.ds(o * R, R)], lvs.at[l, o])
        for l in range(2) for o in range(2)
    ]
    for cp in lv_loads:
        cp.start()
    ev_loads = [
        pltpu.make_async_copy(evaluate.at[q, 0], ev.at[:, pl.ds(q * R, R)], evs.at[q]) for q in range(2)
    ]
    for cp in ev_loads:
        cp.start()

    greet = [x_dev(d, e) for d, e in others] + level_dev + [z_dev, near_dev[1]]
    barrier = pltpu.get_barrier_semaphore()
    for dev in greet:
        pl.semaphore_signal(barrier, 1, device_id=dev, device_id_type=MESH)
    left, own, right = near[0, 0], near[0, 1], near[0, 2]
    nlv[0] = jnp.full((8, 128), jnp.where(c == 1, left, right), jnp.int32)
    nlv[1] = jnp.full((8, 128), jnp.where(c == 1, right, left), jnp.int32)
    pl.semaphore_wait(barrier, len(greet))
    nl_cp = [remote(nlv.at[i], nlr.at[i], nl_s.at[i], nl_r.at[i], near_dev[i]) for i in (1, 0)][::-1]

    w_cp = {}
    own_w = []
    for h in range(2):
        col = (x * 4 + h * 2 + c) * KB
        own_w.append(pltpu.make_async_copy(
            transfer.at[:, 0, :, pl.ds(pl.multiple_of(col, KB), KB)],
            w.at[:, pl.ds(0, R), pl.ds(h * KB, KB)], w_s.at[0, h]))

    def send_w(d, e):
        core = c if e == 0 else 1 - c
        slot = ((-d) % 4) * 2 + e
        for h in range(2):
            col = (((x + d) % 4) * 4 + h * 2 + core) * KB
            w_cp[slot, h] = remote(
                transfer.at[:, 0, :, pl.ds(pl.multiple_of(col, KB), KB)],
                w.at[:, pl.ds(slot * R, R), pl.ds(h * KB, KB)],
                w_s.at[slot, h], w_r.at[slot, h], x_dev(d, e))

    l_cp = {}

    def send_level(l, b):
        l_cp[l, b] = remote(
            v.at[l, b, :, pl.ds(0, R), :], v.at[l, b, :, pl.ds(R, R), :], l_s.at[l, b], l_r.at[l, b], level_dev[l])

    for b in range(SBLK):
        for cp in loads[b]:
            cp.wait()
        re, im = cdot(an[0, b], an[1, b], ch[0, b], ch[1, b])
        v[0, b, 0, pl.ds(0, R), :] = re.astype(BF16)
        v[0, b, 1, pl.ds(0, R), :] = im.astype(BF16)
        send_level(0, b)

    for d, e in others:
        send_w(d, e)
    for cp in own_w:
        cp.start()

    nm = {}
    for i in (1, 0):
        nl_cp[i].wait_recv()
        nm[i] = pltpu.make_async_copy(nlr.at[i], nlm.at[i], nm_s.at[i])
        nm[i].start()
    xs_cp, n_cp = {}, {}

    def pick(i):
        nm[i].wait()
        index = nlm[i, 0, 0]
        shift = BOX * (2 * c - 1).astype(F32)
        sxs[i, 0:1, :] = sxy[0, pl.ds(index, 1), :] + (shift if i == 0 else -shift)
        sxs[i, 1:2, :] = sxy[1, pl.ds(index, 1), :]

        def some(j, _):
            r = rows_at(j, 64)
            for q in range(2):
                ns[i, q, r, :] = ch[q, index, r, :]
            return 0

        lax.fori_loop(0, PTS // 64, some, 0)
        xs_cp[i] = remote(sxs.at[i], sxr.at[i], xs_s.at[i], xs_r.at[i], near_dev[i])

    def send_near(i, p):
        r = pl.ds(p * PIECE, PIECE)
        n_cp[i, p] = remote(ns.at[i, :, r, :], nr.at[i, :, r, :], n_s.at[i, p], n_r.at[i, p], near_dev[i])

    pick(1)
    for p in FAR_SENDS[0]:
        send_near(1, p)
    pick(0)
    for p in range(NP):
        send_near(0, p)

    amp = 1.0 / (4.0 * math.pi)
    txt[...] = jnp.concatenate([txy[0], txy[1], jnp.zeros((6, PTS), F32)], 0).T
    sxs[2, 0:1, :] = sxy[0, pl.ds(own, 1), :]
    sxs[2, 1:2, :] = sxy[1, pl.ds(own, 1), :]

    def tiles(i, src, scale, first, count):
        def step(j, _):
            at_row = (first + j) * ROWS
            gen_tile(txt, src, scale, at_row, tc.at[i], ts.at[i], at_row)
            return 0
        lax.fori_loop(0, count, step, 0)

    def own_part(first, count):
        def row_step(j, _):
            r = rows_at(first + j, 256)
            acc[0, r, :], acc[1, r, :] = cdot(tc[0, r, :], ts[0, r, :], ch[0, own], ch[1, own])
            return 0
        lax.fori_loop(0, count, row_step, 0)

    def level_step(l, b):
        l_cp[l, b].wait_recv()
        re, im = cdot(lv[l, 0, b], lv[l, 1, b], v[l, b, 0], v[l, b, 1])
        if l == 0:
            v[1, b, 0, pl.ds(0, R), :] = re.astype(BF16)
            v[1, b, 1, pl.ds(0, R), :] = im.astype(BF16)
        else:
            r = pl.ds(pl.multiple_of(hi * KB + b * R, R), R)
            g[0, r, :] = re.astype(BF16)
            g[1, r, :] = im.astype(BF16)

    g_cp = {}
    for cp in lv_loads:
        cp.wait()
    for b in range(SBLK):
        tiles(0, sxs.at[2], amp, 2 * b, 2)
        level_step(0, b)
        send_level(1, b)
        for p in FAR_SENDS[1 + b]:
            send_near(1, p)
    for b in range(SBLK):
        own_part(b, 1)
        level_step(1, b)
        r = pl.ds(pl.multiple_of(hi * KB + b * R, R), R)
        g_cp[b] = remote(g.at[:, r, :], g.at[:, r, :], g_s.at[b], g_r.at[b], z_dev)
        for p in FAR_SENDS[5 + b]:
            send_near(1, p)

    far_amp = jnp.where((t == 0) | (t == 15), 0.0, amp)

    def far_part(p, m=512, done=None):
        cols = pl.ds(p * PIECE, PIECE)

        def row_step(j, _):
            r = rows_at(j, m)
            re, im = cdot(tc[1, r, cols], ts[1, r, cols], nr[1, 0, cols, :], nr[1, 1, cols, :])
            acc[0, r, :] += re
            acc[1, r, :] += im
            if done is not None:
                done(r)
            return 0

        lax.fori_loop(0, PTS // m, row_step, 0)

    xs_cp[0].wait_recv()
    tiles(0, sxr.at[0], amp, 0, 8)
    for p in range(NP):
        n_cp[0, p].wait_recv()

    def sib_step(j, _):
        r = rows_at(j, 256)
        re, im = cdot(tc[0, r, :], ts[0, r, :], nr[0, 0], nr[0, 1])
        acc[0, r, :] += re
        acc[1, r, :] += im
        return 0

    lax.fori_loop(0, PTS // 256, sib_step, 0)
    xs_cp[1].wait_recv()
    tiles(1, sxr.at[1], far_amp, 0, 8)

    p_cp = {}
    for cp in own_w:
        cp.wait()
    for cp in w_cp.values():
        cp.wait_recv()
    for b in range(SBLK):
        g_cp[b].wait_recv()
    for k in range(NC):
        cols = pl.ds(k * CW, CW)
        for j in (1, 0):
            r = pl.ds(j * 4 * R, 4 * R)
            re, im = cdot(w[0, r, :], w[1, r, :], g[0, :, cols], g[1, :, cols])
            ps[k, pl.ds(4 * j, 4), 0] = re.astype(BF16).reshape(4, R, CW)
            ps[k, pl.ds(4 * j, 4), 1] = im.astype(BF16).reshape(4, R, CW)
            for d, e in others:
                if d // 2 == j:
                    back = ((-d) % 4) * 2 + e
                    slot = d * 2 + e
                    p_cp[k, back] = remote(
                        ps.at[k, slot], pr.at[k, back], p_s.at[k, slot], p_r.at[k, back], x_dev(d, e))

    def middle(k):
        cols = pl.ds(k * CW, CW)
        for d, e in others:
            p_cp[k, d * 2 + e].wait_recv()
        for q in range(2):
            total = ps[k, 0, q].astype(F32)
            for d, e in others:
                total = total + pr[k, d * 2 + e, q].astype(F32)
            if q == 0:
                mid[0, pl.ds(0, R), cols] = total.astype(BF16)
                mid[1, pl.ds(R, R), cols] = total.astype(BF16)
            else:
                mid[0, pl.ds(R, R), cols] = (-total).astype(BF16)
                mid[1, pl.ds(0, R), cols] = total.astype(BF16)

    def far_field():
        def row_step(j, _):
            r = rows_at(j, 512)
            for q in range(2):
                acc[q, r, :] += jnp.dot(ev[r, :], mid[q], preferred_element_type=F32)
            return 0
        lax.fori_loop(0, PTS // 512, row_step, 0)

    for p in range(NP - 1):
        n_cp[1, p].wait_recv()
        far_part(p)
    for cp in ev_loads:
        cp.wait()
    for k in range(NC):
        middle(k)
    far_field()
    n_cp[1, NP - 1].wait_recv()
    outs = []
    cols = pl.ds((NP - 1) * PIECE, PIECE)
    for j in range(4):
        r = pl.ds(j * 256, 256)
        re, im = cdot(tc[1, r, cols], ts[1, r, cols], nr[1, 0, cols, :], nr[1, 1, cols, :])
        acc[0, r, :] += re
        acc[1, r, :] += im
        outs.append(pltpu.make_async_copy(acc.at[:, r, :], out.at[:, 0, r, :], o_s.at[j]))
        outs[j].start()
    for cp in outs:
        cp.wait()
    for cp in pending:
        cp.wait_send()


FAR_SENDS = ((), (), (0,), (1,), (), (), (2,), (), (3,))


def shards(charges, source_xy, target_xy, anterp, levels, transfer, evaluate, near_list):
    vmem = pl.BlockSpec(memory_space=pltpu.VMEM)
    hbm = pl.BlockSpec(memory_space=pl.ANY)
    dma = pltpu.SemaphoreType.DMA
    return pl.pallas_call(
        main_kernel,
        out_shape=jax.ShapeDtypeStruct((2, 1, PTS, NR), F32),
        in_specs=[pl.BlockSpec(memory_space=pltpu.SMEM), vmem, vmem, hbm, hbm, hbm, hbm, hbm],
        out_specs=hbm,
        scratch_shapes=[
            pltpu.VMEM((2, SBLK, PTS, NR), BF16),
            pltpu.VMEM((2, SBLK, R, PTS), BF16),
            pltpu.VMEM((2, 2, SBLK, R, 2 * R), BF16),
            pltpu.VMEM((2, 8 * R, 2 * KB), BF16),
            pltpu.VMEM((2, SBLK, 2, 2 * R, NR), BF16),
            pltpu.VMEM((2, 2 * KB, NR), BF16),
            pltpu.VMEM((NC, 8, 2, R, CW), BF16),
            pltpu.VMEM((NC, 8, 2, R, CW), BF16),
            pltpu.VMEM((2, 2 * R, NR), BF16),
            pltpu.VMEM((PTS, 2 * R), BF16),
            pltpu.VMEM((2, 2, PTS, NR), BF16),
            pltpu.VMEM((2, 2, PTS, NR), BF16),
            pltpu.VMEM((2, 8, 128), jnp.int32),
            pltpu.VMEM((2, 8, 128), jnp.int32),
            pltpu.SMEM((2, 8, 128), jnp.int32),
            pltpu.VMEM((3, 2, PTS), F32),
            pltpu.VMEM((2, 2, PTS), F32),
            pltpu.VMEM((PTS, 8), F32),
            pltpu.VMEM((2, PTS, PTS), BF16),
            pltpu.VMEM((2, PTS, PTS), BF16),
            pltpu.VMEM((2, PTS, NR), F32),
            dma((2, SBLK)), dma((2, 2)), dma((2,)), dma((2,)), dma((2,)), dma((2,)), dma((2,)), dma((2,)),
            dma((8, 2)), dma((8, 2)), dma((2, SBLK)), dma((2, SBLK)), dma((SBLK,)), dma((SBLK,)),
            dma((NC, 8)), dma((NC, 8)), dma((2, NP)), dma((2, NP)), dma((4,)),
        ],
        compiler_params=pltpu.CompilerParams(
            collective_id=0, has_side_effects=True, vmem_limit_bytes=60 * 2**20),
        name="field_kernel",
    )(near_list, source_xy, target_xy, charges, anterp, levels, transfer, evaluate)


def solution(mesh):
    return jax.shard_map(
        shards,
        mesh=mesh,
        in_specs=(
            P(None, ("src", "tgt"), None, None),
            P(None, ("src", "tgt"), None),
            P(None, ("src", "tgt"), None),
            P(None, ("src", "tgt"), None, None),
            P(None, None, None, ("src", "tgt"), None, None),
            P(None, ("src", "tgt"), None, None),
            P(None, ("src", "tgt"), None, None),
            P(("src", "tgt"), None),
        ),
        out_specs=P(None, ("src", "tgt"), None, None),
        check_vma=False,
    )
```

time: 154 us -> 121 us (0.79)
  the two profiles are of different devices: /device:TPU:18 before, /device:TPU:1 now
where the time goes in v2:
time: 121 us
  Pallas kernels  116 us (96%)
  local copies, waits for them, and re-layouts  4.64 us (4%)
    pallas_call x1, Pallas kernels, shards(): pl.pallas_call(main_kernel, out_shape=jax.ShapeDtypeStruct((2, 1, PTS, NR...  116 us
    unnamed x1, local copies, waits for them, and re-layouts  4.64 us

profile of v2, /device:TPU:1, one launch (start us, length us, event | category | flops | bytes accessed | tf_op | source)
XLA Modules:
  0.0 120.8 jit_solution(16223033418178098899)
XLA Ops:
  0.0 116.1 %field_kernel.1 = f32[2,1,1024,512]{3,2,1,0:T(8,128)} custom-call(s32[1,3]{1,0:T(1,128)} %near.1, f32[2,4,1024]{2,1,0:T(4,128)} %sxy.1, f32[2,1,1024]{2,1,0:T(1,128)} %txy.1, bf16[2,4,1024,512]{3,2,1,0:T(8,128)(2,1)} %charges.1, bf16[2,4,128,1024]{3,2,1,0:T(8,128)(2,1)} %anterp.1, bf16[2,2,2,4,128,128]{5,4,3,2,1,0:T(8,128)(2,1)} %levels.1, ...), custom_call_target="tpu_custom_call" | custom-call | tf_op jit(solution)/shard_map/field_kernel/pallas_call | solution.py:356
  116.1 4.6 %copy.10 = f32[2,1,1024,512]{3,2,1,0:T(8,128)} copy(f32[2,1,1024,512]{3,2,1,0:T(8,128)} %field_kernel.1) | data formatting | bytes 8388608

commit v3 on v2

--- a/solution.py
+++ b/solution.py
@@ -70,8 +70,8 @@
 
 def main_kernel(
     near, sxy, txy, charges, anterp, levels, transfer, evaluate, out,
-    ch, an, lv, w, v, g, ps, pr, mid, ev, ns, nr, nlv, nlr, nlm, sxs, sxr, txt, tc, ts, acc,
-    ld, lvs, evs, nl_s, nl_r, nm_s, xs_s, xs_r, w_s, w_r, l_s, l_r, g_s, g_r, p_s, p_r, n_s, n_r, o_s,
+    ch, an, lv, w, v, g, qs, qr, pf, ps, pr, mid, ev, ns, nr, nlv, nlr, nlm, sxs, sxr, txt, tc, ts, acc,
+    ld, lvs, evs, nl_s, nl_r, nm_s, xs_s, xs_r, w_s, w_r, l_s, l_r, g_s, g_r, q_s, q_r, p_s, p_r, n_s, n_r, o_s,
 ):
     s, t = lax.axis_index("src"), lax.axis_index("tgt")
     n_src = 8
@@ -138,7 +138,7 @@
 
     def send_w(d, e):
         core = c if e == 0 else 1 - c
-        slot = ((-d) % 4) * 2 + e
+        slot = e * 4 + (-d) % 4
         for h in range(2):
             col = (((x + d) % 4) * 4 + h * 2 + core) * KB
             w_cp[slot, h] = remote(
@@ -278,35 +278,49 @@
     xs_cp[1].wait_recv()
     tiles(1, sxr.at[1], far_amp, 0, 8)
 
-    p_cp = {}
+    q_cp, p_cp = {}, {}
     for cp in own_w:
         cp.wait()
     for cp in w_cp.values():
         cp.wait_recv()
     for b in range(SBLK):
         g_cp[b].wait_recv()
+    for p in FAR_SENDS[9]:
+        send_near(1, p)
+
+    def partial(e, k):
+        cols = pl.ds(k * CW, CW)
+        r = pl.ds(e * 4 * R, 4 * R)
+        return cdot(w[0, r, :], w[1, r, :], g[0, :, cols], g[1, :, cols])
+
+    def for_sibling(k):
+        for q, part in enumerate(partial(1, k)):
+            qs[k, :, q] = part.astype(BF16).reshape(4, R, CW)
+        q_cp[k] = remote(qs.at[k], qr.at[k], q_s.at[k], q_r.at[k], near_dev[0])
+
+    def for_targets(k):
+        for q, part in enumerate(partial(0, k)):
+            pf[q] = part.reshape(4, R, CW)
+        q_cp[k].wait_recv()
+        for q in range(2):
+            ps[k, :, q] = (pf[q] + qr[k, :, q].astype(F32)).astype(BF16)
+        for d in (1, 3, 2):
+            p_cp[k, d] = remote(
+                ps.at[k, d], pr.at[k, 4 - d], p_s.at[k, d], p_r.at[k, 4 - d], x_dev(d, 0))
+
     for k in range(NC):
-        cols = pl.ds(k * CW, CW)
-        for j in (1, 0):
-            r = pl.ds(j * 4 * R, 4 * R)
-            re, im = cdot(w[0, r, :], w[1, r, :], g[0, :, cols], g[1, :, cols])
-            ps[k, pl.ds(4 * j, 4), 0] = re.astype(BF16).reshape(4, R, CW)
-            ps[k, pl.ds(4 * j, 4), 1] = im.astype(BF16).reshape(4, R, CW)
-            for d, e in others:
-                if d // 2 == j:
-                    back = ((-d) % 4) * 2 + e
-                    slot = d * 2 + e
-                    p_cp[k, back] = remote(
-                        ps.at[k, slot], pr.at[k, back], p_s.at[k, slot], p_r.at[k, back], x_dev(d, e))
+        for_sibling(k)
+    for k in range(NC):
+        for_targets(k)
 
     def middle(k):
         cols = pl.ds(k * CW, CW)
-        for d, e in others:
-            p_cp[k, d * 2 + e].wait_recv()
+        for d in (1, 2, 3):
+            p_cp[k, d].wait_recv()
         for q in range(2):
             total = ps[k, 0, q].astype(F32)
-            for d, e in others:
-                total = total + pr[k, d * 2 + e, q].astype(F32)
+            for d in (1, 2, 3):
+                total = total + pr[k, d, q].astype(F32)
             if q == 0:
                 mid[0, pl.ds(0, R), cols] = total.astype(BF16)
                 mid[1, pl.ds(R, R), cols] = total.astype(BF16)
@@ -346,7 +360,7 @@
         cp.wait_send()
 
 
-FAR_SENDS = ((), (), (0,), (1,), (), (), (2,), (), (3,))
+FAR_SENDS = ((), (), (0,), (1,), (), (), (), (), (2,), (3,))
 
 
 def shards(charges, source_xy, target_xy, anterp, levels, transfer, evaluate, near_list):
@@ -365,8 +379,11 @@
             pltpu.VMEM((2, 8 * R, 2 * KB), BF16),
             pltpu.VMEM((2, SBLK, 2, 2 * R, NR), BF16),
             pltpu.VMEM((2, 2 * KB, NR), BF16),
-            pltpu.VMEM((NC, 8, 2, R, CW), BF16),
-            pltpu.VMEM((NC, 8, 2, R, CW), BF16),
+            pltpu.VMEM((NC, 4, 2, R, CW), BF16),
+            pltpu.VMEM((NC, 4, 2, R, CW), BF16),
+            pltpu.VMEM((2, 4, R, CW), F32),
+            pltpu.VMEM((NC, 4, 2, R, CW), BF16),
+            pltpu.VMEM((NC, 4, 2, R, CW), BF16),
             pltpu.VMEM((2, 2 * R, NR), BF16),
             pltpu.VMEM((PTS, 2 * R), BF16),
             pltpu.VMEM((2, 2, PTS, NR), BF16),
@@ -382,7 +399,7 @@
             pltpu.VMEM((2, PTS, NR), F32),
             dma((2, SBLK)), dma((2, 2)), dma((2,)), dma((2,)), dma((2,)), dma((2,)), dma((2,)), dma((2,)),
             dma((8, 2)), dma((8, 2)), dma((2, SBLK)), dma((2, SBLK)), dma((SBLK,)), dma((SBLK,)),
-            dma((NC, 8)), dma((NC, 8)), dma((2, NP)), dma((2, NP)), dma((4,)),
+            dma((NC,)), dma((NC,)), dma((NC, 4)), dma((NC, 4)), dma((2, NP)), dma((2, NP)), dma((4,)),
         ],
         compiler_params=pltpu.CompilerParams(
             collective_id=0, has_side_effects=True, vmem_limit_bytes=60 * 2**20),

time: 121 us -> 112 us (0.926)
  the two profiles are of different devices: /device:TPU:1 before, /device:TPU:2 now
where the time goes in v3:
time: 112 us
  Pallas kernels  107 us (96%)
  local copies, waits for them, and re-layouts  4.64 us (4%)
    pallas_call x1, Pallas kernels, shards(): pl.pallas_call(main_kernel, out_shape=jax.ShapeDtypeStruct((2, 1, PTS, NR...  107 us
    unnamed x1, local copies, waits for them, and re-layouts  4.64 us

profile of v3, /device:TPU:2, one launch (start us, length us, event | category | flops | bytes accessed | tf_op | source)
XLA Modules:
  0.0 112.1 jit_solution(10400840488244111717)
XLA Ops:
  0.0 107.4 %field_kernel.1 = f32[2,1,1024,512]{3,2,1,0:T(8,128)} custom-call(s32[1,3]{1,0:T(1,128)} %near.1, f32[2,4,1024]{2,1,0:T(4,128)} %sxy.1, f32[2,1,1024]{2,1,0:T(1,128)} %txy.1, bf16[2,4,1024,512]{3,2,1,0:T(8,128)(2,1)} %charges.1, bf16[2,4,128,1024]{3,2,1,0:T(8,128)(2,1)} %anterp.1, bf16[2,2,2,4,128,128]{5,4,3,2,1,0:T(8,128)(2,1)} %levels.1, ...), custom_call_target="tpu_custom_call" | custom-call | tf_op jit(solution)/shard_map/field_kernel/pallas_call | solution.py:370
  107.5 4.6 %copy.10 = f32[2,1,1024,512]{3,2,1,0:T(8,128)} copy(f32[2,1,1024,512]{3,2,1,0:T(8,128)} %field_kernel.1) | data formatting | bytes 8388608

commit v4 on v3

--- a/solution.py
+++ b/solution.py
@@ -69,9 +69,9 @@
 
 
 def main_kernel(
-    near, sxy, txy, charges, anterp, levels, transfer, evaluate, out,
-    ch, an, lv, w, v, g, qs, qr, pf, ps, pr, mid, ev, ns, nr, nlv, nlr, nlm, sxs, sxr, txt, tc, ts, acc,
-    ld, lvs, evs, nl_s, nl_r, nm_s, xs_s, xs_r, w_s, w_r, l_s, l_r, g_s, g_r, q_s, q_r, p_s, p_r, n_s, n_r, o_s,
+    near, sxy, txy, charges, anterp, levels, transfer, near_out, tile_out, piece_out, mid,
+    ch, an, lv, w, v, g, qs, qr, pf, ps, pr, ns, nr, rl, nlv, nlr, nlm, sxs, sxr, txt, tc, ts, acc, rounded,
+    ld, lvs, nl_s, nl_r, nm_s, xs_s, xs_r, w_s, w_r, l_s, l_r, g_s, g_r, q_s, q_r, p_s, p_r, n_s, n_r, rl_s, rl_r, o_s,
 ):
     s, t = lax.axis_index("src"), lax.axis_index("tgt")
     n_src = 8
@@ -86,6 +86,14 @@
     level_dev = [at((s + n_src // 2) % n_src, t), at(s // 4 * 4 + (s + 2) % 4, t)]
     z_dev = at(s, x * 4 + (1 - hi) * 2 + c)
 
+    has_far = (t != 0) & (t != 15)
+    relay = jnp.logical_not(has_far)
+    relayed = (t == 3) | (t == 12)
+    crossing = hi == c
+    direct = has_far & jnp.logical_not(relayed)
+    relay_dev = at(s, jnp.where(x == 0, 3 - t, jnp.where(x == 3, 27 - t, t)))
+    relay_target = at(s, jnp.where(x == 0, 4, 11))
+
     def x_dev(d, e):
         core = c if e == 0 else 1 - c
         return at(s, ((x + d) % 4) * 4 + hi * 2 + core)
@@ -93,10 +101,13 @@
     others = [(d, e) for d in (1, 3, 2, 0) for e in (0, 1) if (d, e) != (0, 0)]
     pending = []
 
-    def remote(src, dst, ss, rs, dev):
+    def remote(src, dst, ss, rs, dev, only=None):
         cp = pltpu.make_async_remote_copy(src, dst, ss, rs, device_id=dev, device_id_type=MESH)
-        pending.append(cp)
-        cp.start()
+        pending.append((only, cp))
+        if only is None:
+            cp.start()
+        else:
+            pl.when(only)(cp.start)
         return cp
 
     loads = []
@@ -104,28 +115,38 @@
         loads.append((
             pltpu.make_async_copy(anterp.at[:, b], an.at[:, b], ld.at[1, b]),
             pltpu.make_async_copy(charges.at[:, b], ch.at[:, b], ld.at[0, b])))
-        for cp in loads[b]:
-            cp.start()
+        if b < 2:
+            for cp in loads[b]:
+                cp.start()
     lv_loads = [
         pltpu.make_async_copy(levels.at[l, o], lv.at[l, :, :, :, pl.ds(o * R, R)], lvs.at[l, o])
         for l in range(2) for o in range(2)
     ]
-    for cp in lv_loads:
-        cp.start()
-    ev_loads = [
-        pltpu.make_async_copy(evaluate.at[q, 0], ev.at[:, pl.ds(q * R, R)], evs.at[q]) for q in range(2)
-    ]
-    for cp in ev_loads:
-        cp.start()
 
     greet = [x_dev(d, e) for d, e in others] + level_dev + [z_dev, near_dev[1]]
     barrier = pltpu.get_barrier_semaphore()
     for dev in greet:
         pl.semaphore_signal(barrier, 1, device_id=dev, device_id_type=MESH)
+
+    @pl.when(relay | relayed)
+    def _():
+        pl.semaphore_signal(barrier, 1, device_id=relay_dev, device_id_type=MESH)
+
     left, own, right = near[0, 0], near[0, 1], near[0, 2]
     nlv[0] = jnp.full((8, 128), jnp.where(c == 1, left, right), jnp.int32)
     nlv[1] = jnp.full((8, 128), jnp.where(c == 1, right, left), jnp.int32)
-    pl.semaphore_wait(barrier, len(greet))
+
+    def coefficients(b):
+        for cp in loads[b]:
+            cp.wait()
+        for cp in loads[b + 2] if b + 2 < SBLK else lv_loads if b + 2 == SBLK else ():
+            cp.start()
+        re, im = cdot(an[0, b], an[1, b], ch[0, b], ch[1, b])
+        v[0, b, 0, pl.ds(0, R), :] = re.astype(BF16)
+        v[0, b, 1, pl.ds(0, R), :] = im.astype(BF16)
+
+    coefficients(0)
+    pl.semaphore_wait(barrier, len(greet) + (relay | relayed).astype(jnp.int32))
     nl_cp = [remote(nlv.at[i], nlr.at[i], nl_s.at[i], nl_r.at[i], near_dev[i]) for i in (1, 0)][::-1]
 
     w_cp = {}
@@ -153,11 +174,8 @@
             v.at[l, b, :, pl.ds(0, R), :], v.at[l, b, :, pl.ds(R, R), :], l_s.at[l, b], l_r.at[l, b], level_dev[l])
 
     for b in range(SBLK):
-        for cp in loads[b]:
-            cp.wait()
-        re, im = cdot(an[0, b], an[1, b], ch[0, b], ch[1, b])
-        v[0, b, 0, pl.ds(0, R), :] = re.astype(BF16)
-        v[0, b, 1, pl.ds(0, R), :] = im.astype(BF16)
+        if b > 0:
+            coefficients(b)
         send_level(0, b)
 
     for d, e in others:
@@ -170,7 +188,7 @@
         nl_cp[i].wait_recv()
         nm[i] = pltpu.make_async_copy(nlr.at[i], nlm.at[i], nm_s.at[i])
         nm[i].start()
-    xs_cp, n_cp = {}, {}
+    xs_cp, n_cp, rl_cp = {}, {}, {}
 
     def pick(i):
         nm[i].wait()
@@ -188,13 +206,35 @@
         lax.fori_loop(0, PTS // 64, some, 0)
         xs_cp[i] = remote(sxs.at[i], sxr.at[i], xs_s.at[i], xs_r.at[i], near_dev[i])
 
-    def send_near(i, p):
+    def send_near(i, p, only=None):
         r = pl.ds(p * PIECE, PIECE)
-        n_cp[i, p] = remote(ns.at[i, :, r, :], nr.at[i, :, r, :], n_s.at[i, p], n_r.at[i, p], near_dev[i])
+        n_cp[i, p] = remote(
+            ns.at[i, :, r, :], nr.at[i, :, r, :], n_s.at[i, p], n_r.at[i, p], near_dev[i], only)
+
+    def send_crossing(p):
+        if p < len(RELAYS):
+            send_near(1, p, crossing & direct)
+            r = pl.ds(p * PIECE, PIECE)
+            rl_cp[p] = remote(ns.at[1, :, r, :], rl.at[p], n_s.at[1, p], rl_r.at[p], relay_dev, relayed)
+        else:
+            send_near(1, p, crossing & has_far)
+
+    def pass_on(p):
+        pl.when(relay)(rl_cp[p].wait_recv)
+        r = pl.ds(p * PIECE, PIECE)
+        remote(rl.at[p], nr.at[1, :, r, :], rl_s.at[p], n_r.at[1, p], relay_target, relay)
+
+    def sends_at(place):
+        for p in X_SENDS[place]:
+            send_crossing(p)
+        for p in Z_SENDS[place]:
+            send_near(1, p, jnp.logical_not(crossing))
+        for p, where in enumerate(RELAYS):
+            if where == place:
+                pass_on(p)
 
     pick(1)
-    for p in FAR_SENDS[0]:
-        send_near(1, p)
+    sends_at(0)
     pick(0)
     for p in range(NP):
         send_near(0, p)
@@ -236,31 +276,28 @@
         tiles(0, sxs.at[2], amp, 2 * b, 2)
         level_step(0, b)
         send_level(1, b)
-        for p in FAR_SENDS[1 + b]:
-            send_near(1, p)
+        sends_at(1 + b)
     for b in range(SBLK):
         own_part(b, 1)
         level_step(1, b)
         r = pl.ds(pl.multiple_of(hi * KB + b * R, R), R)
         g_cp[b] = remote(g.at[:, r, :], g.at[:, r, :], g_s.at[b], g_r.at[b], z_dev)
-        for p in FAR_SENDS[5 + b]:
-            send_near(1, p)
+        sends_at(5 + b)
 
     far_amp = jnp.where((t == 0) | (t == 15), 0.0, amp)
 
-    def far_part(p, m=512, done=None):
+    def far_part(p):
         cols = pl.ds(p * PIECE, PIECE)
 
         def row_step(j, _):
-            r = rows_at(j, m)
+            r = rows_at(j, 512)
             re, im = cdot(tc[1, r, cols], ts[1, r, cols], nr[1, 0, cols, :], nr[1, 1, cols, :])
             acc[0, r, :] += re
             acc[1, r, :] += im
-            if done is not None:
-                done(r)
             return 0
 
-        lax.fori_loop(0, PTS // m, row_step, 0)
+        n_cp[1, p].wait_recv()
+        lax.fori_loop(0, PTS // 512, row_step, 0)
 
     xs_cp[0].wait_recv()
     tiles(0, sxr.at[0], amp, 0, 8)
@@ -277,6 +314,13 @@
     lax.fori_loop(0, PTS // 256, sib_step, 0)
     xs_cp[1].wait_recv()
     tiles(1, sxr.at[1], far_amp, 0, 8)
+    last = pl.ds((NP - 1) * PIECE, PIECE)
+    outs = [
+        pltpu.make_async_copy(tc.at[1, :, last], tile_out.at[0], o_s.at[0]),
+        pltpu.make_async_copy(ts.at[1, :, last], tile_out.at[1], o_s.at[1]),
+    ]
+    for cp in outs:
+        cp.start()
 
     q_cp, p_cp = {}, {}
     for cp in own_w:
@@ -285,8 +329,7 @@
         cp.wait_recv()
     for b in range(SBLK):
         g_cp[b].wait_recv()
-    for p in FAR_SENDS[9]:
-        send_near(1, p)
+    sends_at(9)
 
     def partial(e, k):
         cols = pl.ds(k * CW, CW)
@@ -328,50 +371,57 @@
                 mid[0, pl.ds(R, R), cols] = (-total).astype(BF16)
                 mid[1, pl.ds(0, R), cols] = total.astype(BF16)
 
-    def far_field():
-        def row_step(j, _):
-            r = rows_at(j, 512)
-            for q in range(2):
-                acc[q, r, :] += jnp.dot(ev[r, :], mid[q], preferred_element_type=F32)
-            return 0
-        lax.fori_loop(0, PTS // 512, row_step, 0)
-
     for p in range(NP - 1):
-        n_cp[1, p].wait_recv()
-        far_part(p)
-    for cp in ev_loads:
-        cp.wait()
+        pl.when(has_far)(functools.partial(far_part, p))
+    rounded[...] = acc[...].astype(BF16)
+    outs.append(pltpu.make_async_copy(rounded, near_out, o_s.at[2]))
+    outs[2].start()
     for k in range(NC):
         middle(k)
-    far_field()
-    n_cp[1, NP - 1].wait_recv()
-    outs = []
-    cols = pl.ds((NP - 1) * PIECE, PIECE)
-    for j in range(4):
-        r = pl.ds(j * 256, 256)
-        re, im = cdot(tc[1, r, cols], ts[1, r, cols], nr[1, 0, cols, :], nr[1, 1, cols, :])
-        acc[0, r, :] += re
-        acc[1, r, :] += im
-        outs.append(pltpu.make_async_copy(acc.at[:, r, :], out.at[:, 0, r, :], o_s.at[j]))
-        outs[j].start()
+
+    @pl.when(relay)
+    def _():
+        nr[1, :, last, :] = jnp.zeros((2, PIECE, NR), BF16)
+
+    pl.when(has_far)(n_cp[1, NP - 1].wait_recv)
+    outs.append(pltpu.make_async_copy(nr.at[1, :, last, :], piece_out, o_s.at[3]))
+    outs[3].start()
     for cp in outs:
         cp.wait()
-    for cp in pending:
-        cp.wait_send()
-
-
-FAR_SENDS = ((), (), (0,), (1,), (), (), (), (), (2,), (3,))
+    for only, cp in pending:
+        if only is None:
+            cp.wait_send()
+        else:
+            pl.when(only)(cp.wait_send)
+
+
+def finish_kernel(near, tile, piece, mid, evaluate, out):
+    dot = functools.partial(jnp.dot, preferred_element_type=F32)
+    re, im = cdot(tile[0], tile[1], piece[0], piece[1])
+    ev = jnp.concatenate([evaluate[0, 0], evaluate[1, 0]], 1)
+    out[0, 0] = near[0].astype(F32) + re + dot(ev, mid[0])
+    out[1, 0] = near[1].astype(F32) + im + dot(ev, mid[1])
+
+
+RELAYS = (7, 8)
+X_SENDS = ((), (0,), (1,), (2,), (), (3,), (), (), (), ())
+Z_SENDS = ((), (), (), (), (), (), (), (), (0,), (1, 2, 3))
 
 
 def shards(charges, source_xy, target_xy, anterp, levels, transfer, evaluate, near_list):
     vmem = pl.BlockSpec(memory_space=pltpu.VMEM)
     hbm = pl.BlockSpec(memory_space=pl.ANY)
     dma = pltpu.SemaphoreType.DMA
-    return pl.pallas_call(
+    near, tile, piece, mid = pl.pallas_call(
         main_kernel,
-        out_shape=jax.ShapeDtypeStruct((2, 1, PTS, NR), F32),
-        in_specs=[pl.BlockSpec(memory_space=pltpu.SMEM), vmem, vmem, hbm, hbm, hbm, hbm, hbm],
-        out_specs=hbm,
+        out_shape=(
+            jax.ShapeDtypeStruct((2, PTS, NR), BF16),
+            jax.ShapeDtypeStruct((2, PTS, PIECE), BF16),
+            jax.ShapeDtypeStruct((2, PIECE, NR), BF16),
+            jax.ShapeDtypeStruct((2, 2 * R, NR), BF16),
+        ),
+        in_specs=[pl.BlockSpec(memory_space=pltpu.SMEM), vmem, vmem, hbm, hbm, hbm, hbm],
+        out_specs=(hbm, hbm, hbm, vmem),
         scratch_shapes=[
             pltpu.VMEM((2, SBLK, PTS, NR), BF16),
             pltpu.VMEM((2, SBLK, R, PTS), BF16),
@@ -384,10 +434,9 @@
             pltpu.VMEM((2, 4, R, CW), F32),
             pltpu.VMEM((NC, 4, 2, R, CW), BF16),
             pltpu.VMEM((NC, 4, 2, R, CW), BF16),
-            pltpu.VMEM((2, 2 * R, NR), BF16),
-            pltpu.VMEM((PTS, 2 * R), BF16),
             pltpu.VMEM((2, 2, PTS, NR), BF16),
             pltpu.VMEM((2, 2, PTS, NR), BF16),
+            pltpu.VMEM((2, 2, PIECE, NR), BF16),
             pltpu.VMEM((2, 8, 128), jnp.int32),
             pltpu.VMEM((2, 8, 128), jnp.int32),
             pltpu.SMEM((2, 8, 128), jnp.int32),
@@ -397,14 +446,31 @@
             pltpu.VMEM((2, PTS, PTS), BF16),
             pltpu.VMEM((2, PTS, PTS), BF16),
             pltpu.VMEM((2, PTS, NR), F32),
-            dma((2, SBLK)), dma((2, 2)), dma((2,)), dma((2,)), dma((2,)), dma((2,)), dma((2,)), dma((2,)),
+            pltpu.VMEM((2, PTS, NR), BF16),
+            dma((2, SBLK)), dma((2, 2)), dma((2,)), dma((2,)), dma((2,)), dma((2,)), dma((2,)),
             dma((8, 2)), dma((8, 2)), dma((2, SBLK)), dma((2, SBLK)), dma((SBLK,)), dma((SBLK,)),
-            dma((NC,)), dma((NC,)), dma((NC, 4)), dma((NC, 4)), dma((2, NP)), dma((2, NP)), dma((4,)),
+            dma((NC,)), dma((NC,)), dma((NC, 4)), dma((NC, 4)), dma((2, NP)), dma((2, NP)), dma((2,)), dma((2,)), dma((4,)),
         ],
         compiler_params=pltpu.CompilerParams(
             collective_id=0, has_side_effects=True, vmem_limit_bytes=60 * 2**20),
         name="field_kernel",
-    )(near_list, source_xy, target_xy, charges, anterp, levels, transfer, evaluate)
+    )(near_list, source_xy, target_xy, charges, anterp, levels, transfer)
+    rows = 256
+    return pl.pallas_call(
+        finish_kernel,
+        grid=(PTS // rows,),
+        out_shape=jax.ShapeDtypeStruct((2, 1, PTS, NR), F32),
+        in_specs=[
+            pl.BlockSpec((2, rows, NR), lambda i: (0, i, 0)),
+            pl.BlockSpec((2, rows, PIECE), lambda i: (0, i, 0)),
+            pl.BlockSpec((2, PIECE, NR), lambda i: (0, 0, 0)),
+            pl.BlockSpec((2, 2 * R, NR), lambda i: (0, 0, 0)),
+            pl.BlockSpec((2, 1, rows, R), lambda i: (0, 0, i, 0)),
+        ],
+        out_specs=pl.BlockSpec((2, 1, rows, NR), lambda i: (0, 0, i, 0)),
+        compiler_params=pltpu.CompilerParams(vmem_limit_bytes=60 * 2**20),
+        name="finish_kernel",
+    )(near, tile, piece, mid, evaluate)
 
 
 def solution(mesh):

time: 112 us -> 111 us (level)
  the two profiles are of different devices: /device:TPU:2 before, /device:TPU:7 now
where the time goes in v4:
time: 111 us; the launch traced here: 110 us
  Pallas kernels  110 us (99%)
    pallas_call x1, Pallas kernels, shards(): pl.pallas_call(main_kernel, out_shape=(jax.ShapeDtypeStruct((2, PTS, NR),...  104 us
    pallas_call x1, Pallas kernels, shards(): pl.pallas_call(finish_kernel, grid=(PTS // rows,), out_shape=jax.ShapeDty...  5.88 us

profile of v4, /device:TPU:7, one launch (start us, length us, event | category | flops | bytes accessed | tf_op | source)
XLA Modules:
  0.0 110.4 jit_solution(12593841985013840408)
XLA Ops:
  0.0 104.5 %field_kernel.1 = (bf16[2,1024,512]{2,1,0:T(8,128)(2,1)}, bf16[2,1024,256]{2,1,0:T(8,128)(2,1)}, bf16[2,256,512]{2,1,0:T(8,128)(2,1)}, bf16[2,256,512]{2,1,0:T(8,128)(2,1)}) custom-call(s32[1,3]{1,0:T(1,128)} %near.1, f32[2,4,1024]{2,1,0:T(4,128)} %sxy.1, f32[2,1,1024]{2,1,0:T(1,128)} %txy.1, bf16[2,4,1024,512]{3,2,1,0:T(8,128)(2,1)} %charges.1, ...), custom_call_target="tpu_custom_call" | custom-call | tf_op jit(solution)/shard_map/field_kernel/pallas_call | solution.py:415
  104.5 5.9 %finish_kernel.1 = f32[2,1,1024,512]{3,2,1,0:T(8,128)} custom-call(bf16[2,1024,512]{2,1,0:T(8,128)(2,1)} %get-tuple-element.9.near, bf16[2,1024,256]{2,1,0:T(8,128)(2,1)} %get-tuple-element.10.tile, bf16[2,256,512]{2,1,0:T(8,128)(2,1)} %get-tuple-element.11.piece, bf16[2,256,512]{2,1,0:T(8,128)(2,1)} %get-tuple-element.12.mid, bf16[2,1,1024,128]{3,2,1,0:T(8,128)(2,1)} %evaluate.1), custom_call_target="tpu_custom_call" | custom-call | tf_op jit(solution)/shard_map/finish_kernel/pallas_call | solution.py:459

commit v5 on v4

--- a/solution.py
+++ b/solution.py
@@ -395,12 +395,39 @@
             pl.when(only)(cp.wait_send)
 
 
-def finish_kernel(near, tile, piece, mid, evaluate, out):
+def finish_kernel(near, tile, piece, mid, evaluate, out, nv, tv, pv, mv, ev, ov, n_l, t_l, p_l, m_l, e_l, o_s):
     dot = functools.partial(jnp.dot, preferred_element_type=F32)
-    re, im = cdot(tile[0], tile[1], piece[0], piece[1])
-    ev = jnp.concatenate([evaluate[0, 0], evaluate[1, 0]], 1)
-    out[0, 0] = near[0].astype(F32) + re + dot(ev, mid[0])
-    out[1, 0] = near[1].astype(F32) + im + dot(ev, mid[1])
+    steps = n_l.shape[0]
+    rows = PTS // steps
+    whole = [pltpu.make_async_copy(piece, pv, p_l), pltpu.make_async_copy(mid, mv, m_l)]
+    loads = []
+    for j in range(steps):
+        r = pl.ds(j * rows, rows)
+        loads.append([
+            pltpu.make_async_copy(tile.at[:, r, :], tv.at[:, r, :], t_l.at[j]),
+            pltpu.make_async_copy(evaluate.at[:, 0, r, :], ev.at[:, r, :], e_l.at[j]),
+            pltpu.make_async_copy(near.at[:, r, :], nv.at[:, r, :], n_l.at[j]),
+        ])
+    for cp in whole + [cp for load in loads for cp in load]:
+        cp.start()
+    for cp in whole:
+        cp.wait()
+    stores = []
+    for j in range(steps):
+        for cp in loads[j]:
+            cp.wait()
+        r = pl.ds(j * rows, rows)
+        er_ei = jnp.concatenate([ev[0, r, :], ev[1, r, :]], 1)
+        for q in range(2):
+            if q == 0:
+                part = dot(tv[0, r, :], pv[0]) - dot(tv[1, r, :], pv[1])
+            else:
+                part = dot(tv[0, r, :], pv[1]) + dot(tv[1, r, :], pv[0])
+            ov[q, r, :] = nv[q, r, :].astype(F32) + part + dot(er_ei, mv[q])
+            stores.append(pltpu.make_async_copy(ov.at[q, r, :], out.at[q, 0, r, :], o_s.at[j, q]))
+            stores[-1].start()
+    for cp in stores:
+        cp.wait()
 
 
 RELAYS = (7, 8)
@@ -455,19 +482,21 @@
             collective_id=0, has_side_effects=True, vmem_limit_bytes=60 * 2**20),
         name="field_kernel",
     )(near_list, source_xy, target_xy, charges, anterp, levels, transfer)
-    rows = 256
+    steps = 2
     return pl.pallas_call(
         finish_kernel,
-        grid=(PTS // rows,),
         out_shape=jax.ShapeDtypeStruct((2, 1, PTS, NR), F32),
-        in_specs=[
-            pl.BlockSpec((2, rows, NR), lambda i: (0, i, 0)),
-            pl.BlockSpec((2, rows, PIECE), lambda i: (0, i, 0)),
-            pl.BlockSpec((2, PIECE, NR), lambda i: (0, 0, 0)),
-            pl.BlockSpec((2, 2 * R, NR), lambda i: (0, 0, 0)),
-            pl.BlockSpec((2, 1, rows, R), lambda i: (0, 0, i, 0)),
+        in_specs=[hbm] * 5,
+        out_specs=hbm,
+        scratch_shapes=[
+            pltpu.VMEM((2, PTS, NR), BF16),
+            pltpu.VMEM((2, PTS, PIECE), BF16),
+            pltpu.VMEM((2, PIECE, NR), BF16),
+            pltpu.VMEM((2, 2 * R, NR), BF16),
+            pltpu.VMEM((2, PTS, R), BF16),
+            pltpu.VMEM((2, PTS, NR), F32),
+            dma((steps,)), dma((steps,)), dma, dma, dma((steps,)), dma((steps, 2)),
         ],
-        out_specs=pl.BlockSpec((2, 1, rows, NR), lambda i: (0, 0, i, 0)),
         compiler_params=pltpu.CompilerParams(vmem_limit_bytes=60 * 2**20),
         name="finish_kernel",
     )(near, tile, piece, mid, evaluate)

time: 111 us -> 110 us (level)
  no operation moved by 1% of the time
where the time goes in v5:
time: 110 us; the launch traced here: 109 us
  Pallas kernels  109 us (99%)
    pallas_call x1, Pallas kernels, shards(): pl.pallas_call(main_kernel, out_shape=(jax.ShapeDtypeStruct((2, PTS, NR),...  104 us
    pallas_call x1, Pallas kernels, shards(): pl.pallas_call(finish_kernel, out_shape=jax.ShapeDtypeStruct((2, 1, PTS,...  4.83 us

profile of v5, /device:TPU:7, one launch (start us, length us, event | category | flops | bytes accessed | tf_op | source)
XLA Modules:
  0.0 109.5 jit_solution(12601239967236717746)
XLA Ops:
  0.0 104.5 %field_kernel.1 = (bf16[2,1024,512]{2,1,0:T(8,128)(2,1)}, bf16[2,1024,256]{2,1,0:T(8,128)(2,1)}, bf16[2,256,512]{2,1,0:T(8,128)(2,1)}, bf16[2,256,512]{2,1,0:T(8,128)(2,1)}) custom-call(s32[1,3]{1,0:T(1,128)} %near.1, f32[2,4,1024]{2,1,0:T(4,128)} %sxy.1, f32[2,1,1024]{2,1,0:T(1,128)} %txy.1, bf16[2,4,1024,512]{3,2,1,0:T(8,128)(2,1)} %charges.1, ...), custom_call_target="tpu_custom_call" | custom-call | tf_op jit(solution)/shard_map/field_kernel/pallas_call | solution.py:442
  104.5 4.8 %finish_kernel.1 = f32[2,1,1024,512]{3,2,1,0:T(8,128)} custom-call(bf16[2,1024,512]{2,1,0:T(8,128)(2,1)} %get-tuple-element.9.near, bf16[2,1024,256]{2,1,0:T(8,128)(2,1)} %get-tuple-element.10.tile, bf16[2,256,512]{2,1,0:T(8,128)(2,1)} %get-tuple-element.11.piece, bf16[2,256,512]{2,1,0:T(8,128)(2,1)} %get-tuple-element.12.mid, bf16[2,1,1024,128]{3,2,1,0:T(8,128)(2,1)} %evaluate.1), custom_call_target="tpu_custom_call" | custom-call | tf_op jit(solution)/shard_map/finish_kernel/pallas_call | solution.py:486

commit v6 on v5

--- a/solution.py
+++ b/solution.py
@@ -301,6 +301,7 @@
 
     xs_cp[0].wait_recv()
     tiles(0, sxr.at[0], amp, 0, 8)
+    sends_at(10)
     for p in range(NP):
         n_cp[0, p].wait_recv()
 
@@ -312,6 +313,7 @@
         return 0
 
     lax.fori_loop(0, PTS // 256, sib_step, 0)
+    sends_at(11)
     xs_cp[1].wait_recv()
     tiles(1, sxr.at[1], far_amp, 0, 8)
     last = pl.ds((NP - 1) * PIECE, PIECE)
@@ -431,8 +433,8 @@
 
 
 RELAYS = (7, 8)
-X_SENDS = ((), (0,), (1,), (2,), (), (3,), (), (), (), ())
-Z_SENDS = ((), (), (), (), (), (), (), (), (0,), (1, 2, 3))
+X_SENDS = ((), (0,), (1,), (2,), (), (3,), (), (), (), (), (), ())
+Z_SENDS = ((), (), (), (), (), (), (), (), (0,), (3,), (1,), (2,))
 
 
 def shards(charges, source_xy, target_xy, anterp, levels, transfer, evaluate, near_list):

time: 110 us -> 110 us (level)
  no operation moved by 1% of the time
where the time goes in v6:
time: 110 us; the launch traced here: 109 us
  Pallas kernels  109 us (99%)
    pallas_call x1, Pallas kernels, shards(): pl.pallas_call(main_kernel, out_shape=(jax.ShapeDtypeStruct((2, PTS, NR),...  104 us
    pallas_call x1, Pallas kernels, shards(): pl.pallas_call(finish_kernel, out_shape=jax.ShapeDtypeStruct((2, 1, PTS,...  4.83 us

profile of v6, /device:TPU:7, one launch (start us, length us, event | category | flops | bytes accessed | tf_op | source)
XLA Modules:
  0.0 109.5 jit_solution(2710858972079685900)
XLA Ops:
  0.0 104.5 %field_kernel.1 = (bf16[2,1024,512]{2,1,0:T(8,128)(2,1)}, bf16[2,1024,256]{2,1,0:T(8,128)(2,1)}, bf16[2,256,512]{2,1,0:T(8,128)(2,1)}, bf16[2,256,512]{2,1,0:T(8,128)(2,1)}) custom-call(s32[1,3]{1,0:T(1,128)} %near.1, f32[2,4,1024]{2,1,0:T(4,128)} %sxy.1, f32[2,1,1024]{2,1,0:T(1,128)} %txy.1, bf16[2,4,1024,512]{3,2,1,0:T(8,128)(2,1)} %charges.1, ...), custom_call_target="tpu_custom_call" | custom-call | tf_op jit(solution)/shard_map/field_kernel/pallas_call | solution.py:444
  104.5 4.8 %finish_kernel.1 = f32[2,1,1024,512]{3,2,1,0:T(8,128)} custom-call(bf16[2,1024,512]{2,1,0:T(8,128)(2,1)} %get-tuple-element.9.near, bf16[2,1024,256]{2,1,0:T(8,128)(2,1)} %get-tuple-element.10.tile, bf16[2,256,512]{2,1,0:T(8,128)(2,1)} %get-tuple-element.11.piece, bf16[2,256,512]{2,1,0:T(8,128)(2,1)} %get-tuple-element.12.mid, bf16[2,1,1024,128]{3,2,1,0:T(8,128)(2,1)} %evaluate.1), custom_call_target="tpu_custom_call" | custom-call | tf_op jit(solution)/shard_map/finish_kernel/pallas_call | solution.py:488
